TPU v7x, 256 devices: a whole 4x4x8 slice. The times are simulated.
256 devices in a mesh: ep: 32 (over x, y, core), etp: 8 (over z).
Axes of the slice: x: 4, y: 4, z: 8, core: 2. Of those that a mesh axis runs over, the one named last changes fastest.
Arguments:
- tokens: bfloat16 [4096, 3584], P('ep'), may hold values from -6 to 6
- out_grad: bfloat16 [4096, 3584], P('ep'), may hold values from -6 to 6
- expert_ids: int32 [4096, 2], P('ep'), may hold values from 0 to 31, as said below
- route_probs: bfloat16 [4096, 2], P('ep'), may hold values from 0.099609375 to 1
- w_gate: bfloat16 [32, 3584, 3200], P('ep', None, 'etp'), may hold values from -0.09375 to 0.09375
- w_up: bfloat16 [32, 3584, 3200], P('ep', None, 'etp'), may hold values from -0.09375 to 0.09375
- w_down: bfloat16 [32, 3200, 3584], P('ep', 'etp'), may hold values from -0.109375 to 0.109375
Outputs:
- token_grad: bfloat16 [4096, 3584], P('ep')
- prob_grad: bfloat16 [4096, 2], P('ep')
- down_grad: bfloat16 [32, 3200, 3584], P('ep', 'etp')
Inputs may be any that keep to these rules, and one draw needn't show every extreme that they name: `expert_ids`: each row names two different experts. Among the 128 rows of one device (aligned blocks of rows) no expert is named more than 16 times, and in every draw one expert is named exactly 16 times within the rows of every device.
All inputs are finite; a program needn't handle non-finite values.
Results may differ from a plain program's by a relative error of at most 0.02.
Values may be sent and summed in bfloat16 or wider, within the bound.
No kernel may reach another device: no remote copies, remote signals or barrier semaphores. Data moves between devices by JAX's collectives and lax.ppermute only.
A program may use at most 128 MiB of HBM per device.

v0:
```python
import functools

import jax
import jax.numpy as jnp
from jax import lax
from jax.experimental import pallas as pl
from jax.experimental.pallas import tpu as pltpu
from jax.sharding import PartitionSpec as P

D = 3584
UNITS = 400
TOK = 128
EXPERTS = 32
N_Z = 8
ROWS = 256
QUARTER = D // 4
WIDE = 384
PACK = 2 * WIDE + 128
BF = jnp.bfloat16
F32 = jnp.float32

NT = (((1,), (1,)), ((), ()))
TN = (((0,), (0,)), ((), ()))
NN = (((1,), (0,)), ((), ()))


def mm(left, right, dims=NN):
    return lax.dot_general(left, right, dims, preferred_element_type=F32)


def params(mib=20):
    return pltpu.CompilerParams(vmem_limit_bytes=mib * 2**20)


VM = pl.BlockSpec(memory_space=pltpu.VMEM)
SM = pl.BlockSpec(memory_space=pltpu.SMEM)
HBM = pl.BlockSpec(memory_space=pltpu.HBM)


def slots_of(ids_ref):
    expert = lax.broadcasted_iota(jnp.int32, (EXPERTS, TOK), 0)
    first = ids_ref[0:1, :]
    second = ids_ref[1:2, :]
    hot0 = (expert == first).astype(F32)
    hot1 = (expert == second).astype(F32)
    earlier = lax.broadcasted_iota(jnp.int32, (TOK, TOK), 0) < lax.broadcasted_iota(
        jnp.int32, (TOK, TOK), 1
    )
    before = earlier.astype(BF)
    rank0 = mm(hot0.astype(BF), before)
    rank1 = mm(hot1.astype(BF), before) + jnp.sum(hot0, axis=1, keepdims=True)
    pos0 = jnp.sum(hot0 * rank0, axis=0, keepdims=True).astype(jnp.int32)
    pos1 = jnp.sum(hot1 * rank1, axis=0, keepdims=True).astype(jnp.int32)
    return first * 16 + pos0, second * 16 + pos1


def row_hot(slot, half):
    row = lax.broadcasted_iota(jnp.int32, (ROWS, TOK), 0)
    return ((row >> 3) * 16 + half * 8 + (row & 7)) == slot


def hot_of(slots, half):
    return jnp.logical_or(row_hot(slots[0], half), row_hot(slots[1], half)).astype(BF)


def prob_of(slots, prob_ref, half):
    weight = jnp.zeros((ROWS, TOK), F32)
    for k in range(2):
        weight += jnp.where(row_hot(slots[k], half), prob_ref[k : k + 1, :].astype(F32), 0.0)
    return jnp.sum(weight, axis=1, keepdims=True)


def send_ring_kernel(
    z_ref, ids_hbm, prob_hbm, tok_hbm, grad_hbm, out_ref, ids_ref, prob_ref, buf, sems
):
    z = z_ref[0]
    c_ids = pltpu.make_async_copy(ids_hbm, ids_ref, sems.at[0])
    c_prob = pltpu.make_async_copy(prob_hbm, prob_ref, sems.at[1])
    c_ids.start()
    c_prob.start()
    cols = pl.ds(pl.multiple_of(lax.rem(z, 4) * QUARTER, 128), QUARTER)
    of_tokens = pltpu.make_async_copy(tok_hbm.at[:, cols], buf, sems.at[2])
    of_grads = pltpu.make_async_copy(grad_hbm.at[:, cols], buf, sems.at[2])

    @pl.when(z < 4)
    def _():
        of_tokens.start()

    @pl.when(z >= 4)
    def _():
        of_grads.start()

    c_ids.wait()
    slots = slots_of(ids_ref)
    hot = hot_of(slots, 0)
    c_prob.wait()
    prob = jnp.where(z < 4, 1.0, prob_of(slots, prob_ref, 0))
    of_tokens.wait()
    out_ref[...] = (mm(hot, buf[...]) * prob).astype(BF)


def send_plane_kernel(
    ids_hbm, prob_hbm, tok_hbm, grad_hbm, out_ref, ids_ref, prob_ref, tok_ref, grad_ref, sems
):
    copies = [
        pltpu.make_async_copy(src, dst, sems.at[i])
        for i, (src, dst) in enumerate(
            ((ids_hbm, ids_ref), (prob_hbm, prob_ref), (tok_hbm, tok_ref), (grad_hbm, grad_ref))
        )
    ]
    for c in copies:
        c.start()
    copies[0].wait()
    slots = slots_of(ids_ref)
    hot = hot_of(slots, 1)
    copies[1].wait()
    prob = prob_of(slots, prob_ref, 1)
    copies[2].wait()
    copies[3].wait()
    for c in range(0, D, QUARTER):
        out_ref[:, c : c + QUARTER] = mm(hot, tok_ref[:, c : c + QUARTER]).astype(BF)
        out_ref[:, D + c : D + c + QUARTER] = (
            mm(hot, grad_ref[:, c : c + QUARTER]) * prob
        ).astype(BF)


def quarter(q):
    return pl.ds(q * QUARTER, QUARTER)


def expert_kernel(offsets, z_ref, *refs):
    shards = refs[:16]
    both_hbm, down_hbm, gate_hbm, up_hbm = refs[16:20]
    packs = refs[20:36]
    score_ref, hid_ref, rows_hbm = refs[36:39]
    ring, plane, down_w, gate_w, up_w, gate_grad_ref, up_grad_ref, part = refs[39:47]
    values, stage, ring_sems, sems, out_sems = refs[47:]
    z = z_ref[0]
    c_x, c_rows = (
        pltpu.make_async_copy(both_hbm.at[:, i * D : (i + 1) * D], plane.at[i], sems.at[i])
        for i in range(2)
    )
    c_down, c_gate, c_up = (
        pltpu.make_async_copy(src, dst, sems.at[2 + i])
        for i, (src, dst) in enumerate(
            ((down_hbm, down_w), (gate_hbm, gate_w), (up_hbm, up_w))
        )
    )
    c_x.start()
    c_gate.start()
    by_ring = []
    for chain in range(2):
        here = pl.ds(chain * 128, 128)
        for i, off in enumerate(offsets[chain]):
            owner = lax.rem(z + off + 8, 8)
            cols = pl.ds(pl.multiple_of(lax.rem(owner, 4) * QUARTER, 128), QUARTER)
            by_ring.append(
                pltpu.make_async_copy(
                    shards[8 * chain + i], ring.at[owner // 4, here, cols], ring_sems.at[chain, i]
                )
            )

    def ahead(gate, up, back, base):
        sig = jax.nn.sigmoid(gate)
        hidden = (gate * sig * up).astype(BF)
        here = pl.ds(base, ROWS)
        hid_ref[here, :] = hidden
        up_grad_ref[here, :] = (back * gate * sig).astype(BF)
        gate_grad_ref[here, :] = (back * up * sig * (1.0 + gate * (1.0 - sig))).astype(BF)
        score = jnp.sum(back * hidden.astype(F32), axis=1, keepdims=True)
        score_ref[here, :] = jnp.broadcast_to(score, (ROWS, 128)).astype(BF)

    c_x.wait()
    c_gate.wait()
    c_up.start()
    values[0] = mm(plane[0], gate_w[...], NT)
    c_up.wait()
    c_rows.start()
    c_down.start()
    values[1] = mm(plane[0], up_w[...], NT)
    c_rows.wait()
    c_down.wait()
    for c in by_ring:
        c.start()
    values[2] = mm(plane[1], down_w[...], NT)
    ahead(values[0], values[1], values[2], ROWS)
    for c in by_ring:
        c.wait()
    rows_out = pltpu.make_async_copy(ring.at[1], rows_hbm, out_sems.at[16])
    rows_out.start()
    ahead(
        mm(ring[0], gate_w[...], NT),
        mm(ring[0], up_w[...], NT),
        mm(ring[1], down_w[...], NT),
        0,
    )
    for c in range(0, D, QUARTER):
        part[:, c : c + QUARTER] = (
            mm(gate_grad_ref[...], gate_w[:, c : c + QUARTER])
            + mm(up_grad_ref[...], up_w[:, c : c + QUARTER])
        ).astype(BF)
    lane = lax.broadcasted_iota(jnp.int32, (128, 128), 1)
    out_copies = []
    for r in (4, 5, 3, 6, 2, 7, 1, 0):
        shard = lax.rem(z + r, 8)
        cols = pl.ds(pl.multiple_of(shard * WIDE, 128), WIDE)
        tile = pl.ds(pl.multiple_of((24 + shard // 2) * 128, 128), 128)
        odd = lax.rem(shard, 2) == 1
        for half in range(2):
            i = 8 * half + r
            base = half * ROWS
            stage[i, :, :WIDE] = part[base : base + 128, cols]
            stage[i, :, WIDE : 2 * WIDE] = part[base + 128 : base + 256, cols]
            top = part[base : base + 128, tile].astype(F32)
            bottom = part[base + 128 : base + 256, tile].astype(F32)
            top = jnp.where(odd, pltpu.roll(top, 64, 1), top)
            bottom = jnp.where(odd, bottom, pltpu.roll(bottom, 64, 1))
            stage[i, :, 2 * WIDE :] = jnp.where(lane < 64, top, bottom).astype(BF)
            c = pltpu.make_async_copy(stage.at[i], packs[i], out_sems.at[i])
            c.start()
            out_copies.append(c)
    for c in out_copies:
        c.wait()
    rows_out.wait()


def back_kernel(*refs):
    out_ref = refs[7]
    lane = lax.broadcasted_iota(jnp.int32, (128, 128), 1)
    tiles = []
    for half in range(2):
        own, left, right = refs[3 * half : 3 * half + 3]
        total = (
            own[...].astype(F32) + left[...].astype(F32) + right[...].astype(F32)
        )
        base = half * WIDE
        out_ref[0:128, base : base + WIDE] = total[:, :WIDE].astype(BF)
        out_ref[128:256, base : base + WIDE] = total[:, WIDE : 2 * WIDE].astype(BF)
        tile = total[:, 2 * WIDE :]
        tiles.append((tile, pltpu.roll(tile, 64, 1)))
    (t0, r0), (t1, r1) = tiles
    out_ref[0:128, 2 * WIDE : PACK] = jnp.where(lane < 64, t0, r1).astype(BF)
    out_ref[128:256, 2 * WIDE : PACK] = jnp.where(lane < 64, r0, t1).astype(BF)
    score0, score1 = refs[6][0:ROWS, :], refs[6][ROWS:, :]
    wide = lax.broadcasted_iota(jnp.int32, (ROWS, 128), 1)
    out_ref[:, PACK:] = jnp.where(
        wide == 0, score0.astype(F32), jnp.where(wide == 1, score1.astype(F32), 0.0)
    ).astype(BF)


def token_sum_kernel(ids_ref, got_ref, out_ref):
    slot0, slot1 = slots_of(ids_ref)
    hots = [
        [row_hot(slot, half).astype(BF) for slot in (slot0, slot1)] for half in range(2)
    ]
    both = [h[0] + h[1] for h in hots]
    wide = mm(both[0], got_ref[:, :WIDE], TN) + mm(both[1], got_ref[:, WIDE : 2 * WIDE], TN)
    for k in range(3):
        out_ref[128 * k : 128 * k + 128, :] = wide[:, 128 * k : 128 * k + 128].astype(BF)
    tile = got_ref[:, 2 * WIDE : PACK]
    half_tile = mm(both[0], tile, TN) + pltpu.roll(mm(both[1], tile, TN), 64, 1)
    lane = lax.broadcasted_iota(jnp.int32, (64, 128), 1)
    out_ref[WIDE : WIDE + 64, :] = jnp.where(
        lane < 64, half_tile[:64], pltpu.roll(half_tile[64:], 64, 1)
    ).astype(BF)
    scores = got_ref[:, PACK:]
    row = lax.broadcasted_iota(jnp.int32, (16, 128), 0)
    result = jnp.zeros((16, 128), F32)
    for k in range(2):
        total = mm(scores, hots[0][k], TN)[0:1, :] + mm(scores, hots[1][k], TN)[1:2, :]
        result = jnp.where(row == k, total, result)
    out_ref[WIDE + 64 :, :] = result.astype(BF)


def assemble_kernel(prob_in, all_ref, out_ref, prob_ref):
    for i in range(8):
        for k in range(3):
            c = WIDE * i + 128 * k
            out_ref[:, c : c + 128] = all_ref[i, 128 * k : 128 * k + 128, :]
    lane = lax.broadcasted_iota(jnp.int32, (64, 128), 1)
    for j in range(4):
        c = 8 * WIDE + 128 * j
        even = all_ref[2 * j, WIDE : WIDE + 64, :].astype(F32)
        odd = all_ref[2 * j + 1, WIDE : WIDE + 64, :].astype(F32)
        out_ref[0:64, c : c + 128] = jnp.where(lane < 64, even, pltpu.roll(odd, 64, 1)).astype(BF)
        out_ref[64:128, c : c + 128] = jnp.where(lane < 64, pltpu.roll(even, 64, 1), odd).astype(BF)
    total = all_ref[0, WIDE + 64 :, :].astype(F32)
    for i in range(1, 8):
        total = total + all_ref[i, WIDE + 64 :, :].astype(F32)
    prob_ref[...] = (total[0:2, :] / prob_in[...].astype(F32)).astype(BF)


def down_kernel(hid_ref, rows0, rows1, out_ref):
    out_ref[...] = (
        mm(hid_ref[0:ROWS, :], rows0[...], TN) + mm(hid_ref[ROWS:, :], rows1[...], TN)
    ).astype(BF)


OFFSETS = ((0, -1, 1, -2, 2, -3, 3, -4), (0, 1, -1, 2, -2, 3, -3, 4))


def hop(x, by):
    return lax.ppermute(x, "etp", [(i, (i + by) % N_Z) for i in range(N_Z)])


def ring_gather(x, way):
    shards = [x]
    far = near = x
    for step in range(4):
        far = hop(far, way)
        shards.append(far)
        if step < 3:
            near = hop(near, -way)
            shards.append(near)
    return shards


def add_rows(a, b):
    return (a.astype(F32) + b.astype(F32)).astype(BF)


def ring_scatter(packs, sums, way):
    far, near = sums
    for step in range(3):
        far = hop(add_rows(far, packs[4 - way * (step + 1)]), way)
        if step < 2:
            near = hop(add_rows(near, packs[4 + way * (step + 2)]), -way)
    return far, near


def exchange(x):
    return lax.all_to_all(x, "ep", split_axis=0, concat_axis=0, tiled=True)


def shape(*dims, dtype=BF):
    return jax.ShapeDtypeStruct(dims, dtype)


def on_device(tokens, out_grad, expert_ids, route_probs, w_gate, w_up, w_down):
    z = lax.axis_index("etp").astype(jnp.int32).reshape(1)
    ids = expert_ids.T
    probs = route_probs.T
    gate_w = w_gate[0].T
    up_w = w_up[0].T
    down_w = w_down[0]

    small = [
        pltpu.VMEM((2, TOK), jnp.int32),
        pltpu.VMEM((2, TOK), BF),
    ]
    send_ring = pl.pallas_call(
        send_ring_kernel,
        out_shape=shape(ROWS, QUARTER),
        in_specs=[SM] + [HBM] * 4,
        out_specs=VM,
        scratch_shapes=small + [pltpu.VMEM((TOK, QUARTER), BF), pltpu.SemaphoreType.DMA((3,))],
        compiler_params=params(60),
        name="send_ring",
    )(z, ids, probs, tokens, out_grad)
    got_ring = exchange(send_ring.reshape(EXPERTS, 8, QUARTER)).reshape(ROWS, QUARTER)
    send_plane = pl.pallas_call(
        send_plane_kernel,
        out_shape=shape(ROWS, 2 * D),
        in_specs=[HBM] * 4,
        out_specs=VM,
        scratch_shapes=small
        + [pltpu.VMEM((TOK, D), BF)] * 2
        + [pltpu.SemaphoreType.DMA((4,))],
        compiler_params=params(60),
        name="send_plane",
    )(ids, probs, tokens, out_grad)
    got_plane = exchange(send_plane.reshape(EXPERTS, 8, 2 * D)).reshape(ROWS, 2 * D)
    chains = ring_gather(got_ring[:128], 1) + ring_gather(got_ring[128:], -1)

    *packs, score, hidden, ring_rows = pl.pallas_call(
        functools.partial(expert_kernel, OFFSETS),
        out_shape=[shape(128, PACK)] * 16
        + [shape(2 * ROWS, 128), shape(2 * ROWS, UNITS), shape(ROWS, D)],
        in_specs=[SM] + [HBM] * 20,
        out_specs=[HBM] * 16 + [VM] * 2 + [HBM],
        scratch_shapes=[pltpu.VMEM((2, ROWS, D), BF)] * 2
        + [pltpu.VMEM((UNITS, D), BF)] * 3
        + [pltpu.VMEM((2 * ROWS, UNITS), BF)] * 2
        + [
            pltpu.VMEM((2 * ROWS, D), BF),
            pltpu.VMEM((3, ROWS, UNITS), F32),
            pltpu.VMEM((16, 128, PACK), BF),
            pltpu.SemaphoreType.DMA((2, 8)),
            pltpu.SemaphoreType.DMA((5,)),
            pltpu.SemaphoreType.DMA((17,)),
        ],
        compiler_params=params(60),
        name="expert",
    )(z, *chains, got_plane, down_w, gate_w, up_w)
    packs0, packs1 = packs[:8], packs[8:]
    sums0 = (hop(packs0[4], 1), hop(packs0[5], -1))
    sums1 = (hop(packs1[4], -1), hop(packs1[3], 1))
    back_parts = [
        packs0[0],
        *ring_scatter(packs0, sums0, 1),
        packs1[0],
        *ring_scatter(packs1, sums1, -1),
        score,
    ]

    send_back = pl.pallas_call(
        back_kernel,
        out_shape=shape(ROWS, PACK + 128),
        in_specs=[VM] * 7,
        out_specs=VM,
        compiler_params=params(),
        name="pack_back",
    )(*back_parts)
    got_back = exchange(send_back.reshape(EXPERTS, 8, PACK + 128)).reshape(ROWS, PACK + 128)
    down_grad = pl.pallas_call(
        down_kernel,
        out_shape=shape(UNITS, D),
        grid=(4,),
        in_specs=[
            pl.BlockSpec((2 * ROWS, UNITS), lambda i: (0, 0)),
            pl.BlockSpec((ROWS, QUARTER), lambda i: (0, i)),
            pl.BlockSpec((ROWS, QUARTER), lambda i: (0, 4 + i)),
        ],
        out_specs=pl.BlockSpec((UNITS, QUARTER), lambda i: (0, i)),
        compiler_params=params(),
        name="down_grad",
    )(hidden, ring_rows, got_plane)
    got_back, down_grad = lax.optimization_barrier((got_back, down_grad))
    summed = pl.pallas_call(
        token_sum_kernel,
        out_shape=shape(464, 128),
        in_specs=[VM] * 2,
        out_specs=VM,
        compiler_params=params(),
        name="token_sum",
    )(ids, got_back)
    token_grad, prob_grad = pl.pallas_call(
        assemble_kernel,
        out_shape=[shape(TOK, D), shape(2, TOK)],
        in_specs=[VM] * 2,
        out_specs=[VM] * 2,
        compiler_params=params(),
        name="assemble",
    )(probs, lax.all_gather(summed, "etp", axis=0, tiled=False))
    return (token_grad, prob_grad.T, down_grad[None])


def solution(mesh):
    return jax.shard_map(
        on_device,
        mesh=mesh,
        in_specs=(
            P("ep", None),
            P("ep", None),
            P("ep", None),
            P("ep", None),
            P("ep", None, "etp"),
            P("ep", None, "etp"),
            P("ep", "etp", None),
        ),
        out_specs=(P("ep", None), P("ep", None), P("ep", "etp", None)),
        check_vma=False,
    )
```

profile of v0, /device:TPU:32, one launch (start us, length us, event | category | flops | bytes accessed | tf_op | source)
XLA Modules:
  0.0 183.8 jit_solution(1400996160644577551)
XLA Ops:
  0.6 2.1 %send_ring.1 = bf16[256,896]{1,0:T(8,128)(2,1)} custom-call(s32[1]{0:T(128)} %bitcast.2.z_ref, s32[2,128]{1,0:T(2,128)} %bitcast.24, bf16[2,128]{1,0:T(2,128)(2,1)} %bitcast.27, bf16[128,3584]{1,0:T(8,128)(2,1)} %tok_hbm.3, bf16[128,3584]{1,0:T(8,128)(2,1)} %grad_hbm.3), custom_call_target="tpu_custom_call" | custom-call | tf_op jit(solution)/shard_map/send_ring/pallas_call | solution.py:351
  2.7 7.3 %all-to-all-start = ((bf16[32,8,896]{2,1,0:T(8,128)(2,1)}), bf16[32,8,896]{2,1,0:T(8,128)(2,1)S(1)}, u32[]{:S(2)}, u32[]{:S(2)}) async-start(bf16[32,8,896]{2,1,0:T(8,128)(2,1)} %bitcast.35), calls=%async_computation | async-start | bytes 917504 | tf_op jit(solution)/shard_map/all_to_all | solution.py:332
  10.0 4.4 %send_plane.1 = bf16[256,7168]{1,0:T(8,128)(2,1)} custom-call(s32[2,128]{1,0:T(2,128)} %bitcast.25, bf16[2,128]{1,0:T(2,128)(2,1)} %bitcast.28, bf16[128,3584]{1,0:T(8,128)(2,1)} %tok_hbm.3, bf16[128,3584]{1,0:T(8,128)(2,1)} %grad_hbm.3), custom_call_target="tpu_custom_call" | custom-call | tf_op jit(solution)/shard_map/send_plane/pallas_call | solution.py:361
  14.5 6.1 %all-to-all-done = bf16[32,8,896]{2,1,0:T(8,128)(2,1)S(1)} async-done(((bf16[32,8,896]{2,1,0:T(8,128)(2,1)}), bf16[32,8,896]{2,1,0:T(8,128)(2,1)S(1)}, u32[]{:S(2)}, u32[]{:S(2)}) %all-to-all-start) | async-done | bytes 458784 | tf_op jit(solution)/shard_map/all_to_all | solution.py:332
  20.6 4.8 %all-to-all-start.1 = ((bf16[32,8,7168]{2,1,0:T(8,128)(2,1)}), bf16[32,8,7168]{2,1,0:T(8,128)(2,1)}, u32[]{:S(2)}, u32[]{:S(2)}) async-start(bf16[32,8,7168]{2,1,0:T(8,128)(2,1)} %bitcast.30), calls=%async_computation.1 | async-start | bytes 7340032 | tf_op jit(solution)/shard_map/all_to_all | solution.py:332
  27.6 1.9 %collective-permute-start.8 = (bf16[128,896]{1,0:T(8,128)(2,1)S(1)}, bf16[128,896]{1,0:T(8,128)(2,1)S(1)}, u32[]{:S(2)}, u32[]{:S(2)}) collective-permute-start(bf16[128,896]{1,0:T(8,128)(2,1)S(1)} %get-tuple-element.49.refs_8_), channel_id=1, source_target_pairs={{0,1},{1,2},{2,3},{3,4},{4,5},{5,6},{6,7},{7,0},{8,9},{9,10},{10,1... | collective-permute-start | bytes 688136 | tf_op jit(solution)/shard_map/ppermute | solution.py:303
  29.5 2.0 %collective-permute-start.1 = (bf16[128,896]{1,0:T(8,128)(2,1)S(1)}, bf16[128,896]{1,0:T(8,128)(2,1)S(1)}, u32[]{:S(2)}, u32[]{:S(2)}) collective-permute-start(bf16[128,896]{1,0:T(8,128)(2,1)S(1)} %get-tuple-element.50.refs_0_), channel_id=1, source_target_pairs={{0,7},{1,0},{2,1},{3,2},{4,3},{5,4},{6,5},{7,6},{8,15},{9,8},{10,9... | collective-permute-start | bytes 688136 | tf_op jit(solution)/shard_map/ppermute | solution.py:303
  31.5 2.5 %collective-permute-done.7.refs_9_ = bf16[128,896]{1,0:T(8,128)(2,1)S(1)} collective-permute-done((bf16[128,896]{1,0:T(8,128)(2,1)S(1)}, bf16[128,896]{1,0:T(8,128)(2,1)S(1)}, u32[]{:S(2)}, u32[]{:S(2)}) %collective-permute-start.7) | collective-permute-done | bytes 229408 | tf_op jit(solution)/shard_map/ppermute | solution.py:303
  34.0 3.4 %collective-permute-start.9 = (bf16[128,896]{1,0:T(8,128)(2,1)S(1)}, bf16[128,896]{1,0:T(8,128)(2,1)S(1)}, u32[]{:S(2)}, u32[]{:S(2)}) collective-permute-start(bf16[128,896]{1,0:T(8,128)(2,1)S(1)} %collective-permute-done.7.refs_9_), channel_id=1, source_target_pairs={{0,7},{1,0},{2,1},{3,2},{4,3},{5,4},{6,5},{7,6},{8,15},{9,8},{10,9... | collective-permute-start | bytes 688136 | tf_op jit(solution)/shard_map/ppermute | solution.py:303
  37.9 4.9 %collective-permute-done.8.refs_10_ = bf16[128,896]{1,0:T(8,128)(2,1)S(1)} collective-permute-done((bf16[128,896]{1,0:T(8,128)(2,1)S(1)}, bf16[128,896]{1,0:T(8,128)(2,1)S(1)}, u32[]{:S(2)}, u32[]{:S(2)}) %collective-permute-start.8) | collective-permute-done | bytes 229408 | tf_op jit(solution)/shard_map/ppermute | solution.py:303
  42.8 3.4 %collective-permute-start.3 = (bf16[128,896]{1,0:T(8,128)(2,1)S(1)}, bf16[128,896]{1,0:T(8,128)(2,1)S(1)}, u32[]{:S(2)}, u32[]{:S(2)}) collective-permute-start(bf16[128,896]{1,0:T(8,128)(2,1)S(1)} %collective-permute-done.1.refs_2_), channel_id=1, source_target_pairs={{0,7},{1,0},{2,1},{3,2},{4,3},{5,4},{6,5},{7,6},{8,15},{9,8},{10,9... | collective-permute-start | bytes 688136 | tf_op jit(solution)/shard_map/ppermute | solution.py:303
  46.2 3.1 %collective-permute-start.11 = (bf16[128,896]{1,0:T(8,128)(2,1)S(1)}, bf16[128,896]{1,0:T(8,128)(2,1)S(1)}, u32[]{:S(2)}, u32[]{:S(2)}) collective-permute-start(bf16[128,896]{1,0:T(8,128)(2,1)S(1)} %collective-permute-done.9.refs_11_), channel_id=1, source_target_pairs={{0,7},{1,0},{2,1},{3,2},{4,3},{5,4},{6,5},{7,6},{8,15},{9,8},{10,9... | collective-permute-start | bytes 688136 | tf_op jit(solution)/shard_map/ppermute | solution.py:303
  49.4 3.3 %collective-permute-done.10.refs_12_ = bf16[128,896]{1,0:T(8,128)(2,1)S(1)} collective-permute-done((bf16[128,896]{1,0:T(8,128)(2,1)S(1)}, bf16[128,896]{1,0:T(8,128)(2,1)S(1)}, u32[]{:S(2)}, u32[]{:S(2)}) %collective-permute-start.10) | collective-permute-done | bytes 229408 | tf_op jit(solution)/shard_map/ppermute | solution.py:303
  52.7 3.4 %collective-permute-start.5 = (bf16[128,896]{1,0:T(8,128)(2,1)S(1)}, bf16[128,896]{1,0:T(8,128)(2,1)S(1)}, u32[]{:S(2)}, u32[]{:S(2)}) collective-permute-start(bf16[128,896]{1,0:T(8,128)(2,1)S(1)} %collective-permute-done.3.refs_4_), channel_id=1, source_target_pairs={{0,7},{1,0},{2,1},{3,2},{4,3},{5,4},{6,5},{7,6},{8,15},{9,8},{10,9... | collective-permute-start | bytes 688136 | tf_op jit(solution)/shard_map/ppermute | solution.py:303
  56.0 3.1 %collective-permute-start.13 = (bf16[128,896]{1,0:T(8,128)(2,1)S(1)}, bf16[128,896]{1,0:T(8,128)(2,1)S(1)}, u32[]{:S(2)}, u32[]{:S(2)}) collective-permute-start(bf16[128,896]{1,0:T(8,128)(2,1)S(1)} %collective-permute-done.11.refs_13_), channel_id=1, source_target_pairs={{0,7},{1,0},{2,1},{3,2},{4,3},{5,4},{6,5},{7,6},{8,15},{9,8},{10,9... | collective-permute-start | bytes 688136 | tf_op jit(solution)/shard_map/ppermute | solution.py:303
  59.2 3.6 %collective-permute-done.12.refs_14_ = bf16[128,896]{1,0:T(8,128)(2,1)S(1)} collective-permute-done((bf16[128,896]{1,0:T(8,128)(2,1)S(1)}, bf16[128,896]{1,0:T(8,128)(2,1)S(1)}, u32[]{:S(2)}, u32[]{:S(2)}) %collective-permute-start.12) | collective-permute-done | bytes 229408 | tf_op jit(solution)/shard_map/ppermute | solution.py:303
  64.7 2.4 %collective-permute-done.6.refs_7_ = bf16[128,896]{1,0:T(8,128)(2,1)} collective-permute-done((bf16[128,896]{1,0:T(8,128)(2,1)S(1)}, bf16[128,896]{1,0:T(8,128)(2,1)}, u32[]{:S(2)}, u32[]{:S(2)}) %collective-permute-start.6) | collective-permute-done | bytes 229408 | tf_op jit(solution)/shard_map/ppermute | solution.py:303
  67.1 5.0 %all-to-all-done.1 = bf16[32,8,7168]{2,1,0:T(8,128)(2,1)} async-done(((bf16[32,8,7168]{2,1,0:T(8,128)(2,1)}), bf16[32,8,7168]{2,1,0:T(8,128)(2,1)}, u32[]{:S(2)}, u32[]{:S(2)}) %all-to-all-start.1) | async-done | bytes 3670048 | tf_op jit(solution)/shard_map/all_to_all | solution.py:332
  72.2 19.5 %expert.1 = (bf16[128,896]{1,0:T(8,128)(2,1)}, bf16[128,896]{1,0:T(8,128)(2,1)}, bf16[128,896]{1,0:T(8,128)(2,1)}, bf16[128,896]{1,0:T(8,128)(2,1)}, bf16[128,89...) custom-call(s32[1]{0:T(128)} %bitcast.2.z_ref, ...), custom_call_target="tpu_custom_call" | custom-call | tf_op jit(solution)/shard_map/expert/pallas_call | solution.py:375
  91.7 2.0 %collective-permute-start.14 = (bf16[128,896]{1,0:T(8,128)(2,1)}, bf16[128,896]{1,0:T(8,128)(2,1)S(1)}, u32[]{:S(2)}, u32[]{:S(2)}) collective-permute-start(bf16[128,896]{1,0:T(8,128)(2,1)} %get-tuple-element.27), channel_id=1, source_target_pairs={{0,1},{1,2},{2,3},{3,4},{4,5},{5,6},{6,7},{7,0},{8,9},{9,10},{10,1... | collective-permute-start | bytes 688136 | tf_op jit(solution)/shard_map/ppermute | solution.py:303
  93.8 4.0 %collective-permute-start.21 = (bf16[128,896]{1,0:T(8,128)(2,1)}, bf16[128,896]{1,0:T(8,128)(2,1)S(1)}, u32[]{:S(2)}, u32[]{:S(2)}) collective-permute-start(bf16[128,896]{1,0:T(8,128)(2,1)} %get-tuple-element.35), channel_id=1, source_target_pairs={{0,7},{1,0},{2,1},{3,2},{4,3},{5,4},{6,5},{7,6},{8,15},{9,8},{10,9... | collective-permute-start | bytes 688136 | tf_op jit(solution)/shard_map/ppermute | solution.py:303
  100.7 2.7 %collective-permute-start.15 = (bf16[128,896]{1,0:T(8,128)(2,1)S(1)}, bf16[128,896]{1,0:T(8,128)(2,1)S(1)}, u32[]{:S(2)}, u32[]{:S(2)}) collective-permute-start(bf16[128,896]{1,0:T(8,128)(2,1)S(1)} %add_convert_fusion.9), channel_id=1, source_target_pairs={{0,1},{1,2},{2,3},{3,4},{4,5},{5,6},{6,7},{7,0},{8,9},{9,10},{10,1... | collective-permute-start | bytes 688136 | tf_op jit(solution)/shard_map/ppermute | solution.py:303
  104.4 2.1 %collective-permute-start.19 = (bf16[128,896]{1,0:T(8,128)(2,1)S(1)}, bf16[128,896]{1,0:T(8,128)(2,1)S(1)}, u32[]{:S(2)}, u32[]{:S(2)}) collective-permute-start(bf16[128,896]{1,0:T(8,128)(2,1)S(1)} %add_convert_fusion.6), channel_id=1, source_target_pairs={{0,7},{1,0},{2,1},{3,2},{4,3},{5,4},{6,5},{7,6},{8,15},{9,8},{10,9... | collective-permute-start | bytes 688136 | tf_op jit(solution)/shard_map/ppermute | solution.py:303
  107.6 3.3 %collective-permute-start.22 = (bf16[128,896]{1,0:T(8,128)(2,1)S(1)}, bf16[128,896]{1,0:T(8,128)(2,1)S(1)}, u32[]{:S(2)}, u32[]{:S(2)}) collective-permute-start(bf16[128,896]{1,0:T(8,128)(2,1)S(1)} %add_convert_fusion.4), channel_id=1, source_target_pairs={{0,7},{1,0},{2,1},{3,2},{4,3},{5,4},{6,5},{7,6},{8,15},{9,8},{10,9... | collective-permute-start | bytes 688136 | tf_op jit(solution)/shard_map/ppermute | solution.py:303
  112.0 2.3 %collective-permute-start.16 = (bf16[128,896]{1,0:T(8,128)(2,1)S(1)}, bf16[128,896]{1,0:T(8,128)(2,1)S(1)}, u32[]{:S(2)}, u32[]{:S(2)}) collective-permute-start(bf16[128,896]{1,0:T(8,128)(2,1)S(1)} %add_convert_fusion.8), channel_id=1, source_target_pairs={{0,1},{1,2},{2,3},{3,4},{4,5},{5,6},{6,7},{7,0},{8,9},{9,10},{10,1... | collective-permute-start | bytes 688136 | tf_op jit(solution)/shard_map/ppermute | solution.py:303
  117.0 3.5 %collective-permute-start.23 = (bf16[128,896]{1,0:T(8,128)(2,1)S(1)}, bf16[128,896]{1,0:T(8,128)(2,1)S(1)}, u32[]{:S(2)}, u32[]{:S(2)}) collective-permute-start(bf16[128,896]{1,0:T(8,128)(2,1)S(1)} %add_convert_fusion.3), channel_id=1, source_target_pairs={{0,7},{1,0},{2,1},{3,2},{4,3},{5,4},{6,5},{7,6},{8,15},{9,8},{10,9... | collective-permute-start | bytes 688136 | tf_op jit(solution)/shard_map/ppermute | solution.py:303
  121.8 2.7 %collective-permute-done.16 = bf16[128,896]{1,0:T(8,128)(2,1)S(1)} collective-permute-done((bf16[128,896]{1,0:T(8,128)(2,1)S(1)}, bf16[128,896]{1,0:T(8,128)(2,1)S(1)}, u32[]{:S(2)}, u32[]{:S(2)}) %collective-permute-start.16) | collective-permute-done | bytes 229408 | tf_op jit(solution)/shard_map/ppermute | solution.py:303
  130.0 2.5 %collective-permute-done.17.refs_1_ = bf16[128,896]{1,0:T(8,128)(2,1)S(1)} collective-permute-done((bf16[128,896]{1,0:T(8,128)(2,1)S(1)}, bf16[128,896]{1,0:T(8,128)(2,1)S(1)}, u32[]{:S(2)}, u32[]{:S(2)}) %collective-permute-start.17) | collective-permute-done | bytes 229408 | tf_op jit(solution)/shard_map/ppermute | solution.py:303
  135.1 6.0 %all-to-all-start.2 = ((bf16[32,8,1024]{2,1,0:T(8,128)(2,1)}), bf16[32,8,1024]{2,1,0:T(8,128)(2,1)S(1)}, u32[]{:S(2)}, u32[]{:S(2)}) async-start(bf16[32,8,1024]{2,1,0:T(8,128)(2,1)} %bitcast.13), calls=%async_computation.2 | async-start | bytes 1048576 | tf_op jit(solution)/shard_map/all_to_all | solution.py:332
  141.1 5.1 %down_grad.1 = bf16[400,3584]{1,0:T(8,128)(2,1)} custom-call(bf16[512,400]{1,0:T(8,128)(2,1)S(1)} %copy-done.1, bf16[256,3584]{1,0:T(8,128)(2,1)S(1)} %copy-done, bf16[256,7168]{1,0:T(8,128)(2,1)} %bitcast.7.refs_16_.rows1), custom_call_target="tpu_custom_call" | custom-call | tf_op jit(solution)/shard_map/down_grad/pallas_call | solution.py:415
  146.3 6.0 %all-to-all-done.2 = bf16[32,8,1024]{2,1,0:T(8,128)(2,1)S(1)} async-done(((bf16[32,8,1024]{2,1,0:T(8,128)(2,1)}), bf16[32,8,1024]{2,1,0:T(8,128)(2,1)S(1)}, u32[]{:S(2)}, u32[]{:S(2)}) %all-to-all-start.2) | async-done | bytes 524320 | tf_op jit(solution)/shard_map/all_to_all | solution.py:332
  152.9 29.8 %all-gather = bf16[3712,128]{1,0:T(8,128)(2,1)S(1)} all-gather(bf16[464,128]{1,0:T(8,128)(2,1)S(1)} %token_sum.1), channel_id=2, replica_groups=mesh['ep'=32,'etp'=8] {'etp'}, dimensions={0}, use_global_device_ids=true | all-gather | bytes 1069056 | tf_op jit(solution)/shard_map/all_gather | solution.py:444
  (105 shorter events, 24.6 us)
Async XLA Ops:
  2.7 17.9 %all-to-all-start = ((bf16[32,8,896]{2,1,0:T(8,128)(2,1)}), bf16[32,8,896]{2,1,0:T(8,128)(2,1)S(1)}, u32[]{:S(2)}, u32[]{:S(2)}) async-start(bf16[32,8,896]{2,1,0:T(8,128)(2,1)} %bitcast.35), calls=%async_computation | async-start | bytes 917504 | tf_op jit(solution)/shard_map/all_to_all | solution.py:332
  20.6 51.5 %all-to-all-start.1 = ((bf16[32,8,7168]{2,1,0:T(8,128)(2,1)}), bf16[32,8,7168]{2,1,0:T(8,128)(2,1)}, u32[]{:S(2)}, u32[]{:S(2)}) async-start(bf16[32,8,7168]{2,1,0:T(8,128)(2,1)} %bitcast.30), calls=%async_computation.1 | async-start | bytes 7340032 | tf_op jit(solution)/shard_map/all_to_all | solution.py:332
  25.5 46.6 %copy-start.7 = (bf16[128,896]{1,0:T(8,128)(2,1)}, bf16[128,896]{1,0:T(8,128)(2,1)S(1)}, u32[]{:S(2)}) copy-start(bf16[128,896]{1,0:T(8,128)(2,1)S(1)} %get-tuple-element.49.refs_8_) | copy-start | bytes 688132
  25.5 8.6 %collective-permute-start.7 = (bf16[128,896]{1,0:T(8,128)(2,1)S(1)}, bf16[128,896]{1,0:T(8,128)(2,1)S(1)}, u32[]{:S(2)}, u32[]{:S(2)}) collective-permute-start(bf16[128,896]{1,0:T(8,128)(2,1)S(1)} %get-tuple-element.49.refs_8_), channel_id=1, source_target_pairs={{0,7},{1,0},{2,1},{3,2},{4,3},{5,4},{6,5},{7,6},{8,15},{9,8},{10,9... | collective-permute-start | bytes 688136 | tf_op jit(solution)/shard_map/ppermute | solution.py:303
  25.7 12.2 %collective-permute-start = (bf16[128,896]{1,0:T(8,128)(2,1)S(1)}, bf16[128,896]{1,0:T(8,128)(2,1)S(1)}, u32[]{:S(2)}, u32[]{:S(2)}) collective-permute-start(bf16[128,896]{1,0:T(8,128)(2,1)S(1)} %get-tuple-element.50.refs_0_), channel_id=1, source_target_pairs={{0,1},{1,2},{2,3},{3,4},{4,5},{5,6},{6,7},{7,0},{8,9},{9,10},{10,1... | collective-permute-start | bytes 688136 | tf_op jit(solution)/shard_map/ppermute | solution.py:303
  27.6 15.2 %collective-permute-start.8 = (bf16[128,896]{1,0:T(8,128)(2,1)S(1)}, bf16[128,896]{1,0:T(8,128)(2,1)S(1)}, u32[]{:S(2)}, u32[]{:S(2)}) collective-permute-start(bf16[128,896]{1,0:T(8,128)(2,1)S(1)} %get-tuple-element.49.refs_8_), channel_id=1, source_target_pairs={{0,1},{1,2},{2,3},{3,4},{4,5},{5,6},{6,7},{7,0},{8,9},{9,10},{10,1... | collective-permute-start | bytes 688136 | tf_op jit(solution)/shard_map/ppermute | solution.py:303
  29.5 13.3 %collective-permute-start.1 = (bf16[128,896]{1,0:T(8,128)(2,1)S(1)}, bf16[128,896]{1,0:T(8,128)(2,1)S(1)}, u32[]{:S(2)}, u32[]{:S(2)}) collective-permute-start(bf16[128,896]{1,0:T(8,128)(2,1)S(1)} %get-tuple-element.50.refs_0_), channel_id=1, source_target_pairs={{0,7},{1,0},{2,1},{3,2},{4,3},{5,4},{6,5},{7,6},{8,15},{9,8},{10,9... | collective-permute-start | bytes 688136 | tf_op jit(solution)/shard_map/ppermute | solution.py:303
  34.0 12.2 %collective-permute-start.9 = (bf16[128,896]{1,0:T(8,128)(2,1)S(1)}, bf16[128,896]{1,0:T(8,128)(2,1)S(1)}, u32[]{:S(2)}, u32[]{:S(2)}) collective-permute-start(bf16[128,896]{1,0:T(8,128)(2,1)S(1)} %collective-permute-done.7.refs_9_), channel_id=1, source_target_pairs={{0,7},{1,0},{2,1},{3,2},{4,3},{5,4},{6,5},{7,6},{8,15},{9,8},{10,9... | collective-permute-start | bytes 688136 | tf_op jit(solution)/shard_map/ppermute | solution.py:303
  37.9 11.4 %collective-permute-start.2 = (bf16[128,896]{1,0:T(8,128)(2,1)S(1)}, bf16[128,896]{1,0:T(8,128)(2,1)S(1)}, u32[]{:S(2)}, u32[]{:S(2)}) collective-permute-start(bf16[128,896]{1,0:T(8,128)(2,1)S(1)} %collective-permute-done.refs_1_), channel_id=1, source_target_pairs={{0,1},{1,2},{2,3},{3,4},{4,5},{5,6},{6,7},{7,0},{8,9},{9,10},{10,1... | collective-permute-start | bytes 688136 | tf_op jit(solution)/shard_map/ppermute | solution.py:303
  42.8 9.8 %collective-permute-start.10 = (bf16[128,896]{1,0:T(8,128)(2,1)S(1)}, bf16[128,896]{1,0:T(8,128)(2,1)S(1)}, u32[]{:S(2)}, u32[]{:S(2)}) collective-permute-start(bf16[128,896]{1,0:T(8,128)(2,1)S(1)} %collective-permute-done.8.refs_10_), channel_id=1, source_target_pairs={{0,1},{1,2},{2,3},{3,4},{4,5},{5,6},{6,7},{7,0},{8,9},{9,10},{10,1... | collective-permute-start | bytes 688136 | tf_op jit(solution)/shard_map/ppermute | solution.py:303
  42.8 9.8 %collective-permute-start.3 = (bf16[128,896]{1,0:T(8,128)(2,1)S(1)}, bf16[128,896]{1,0:T(8,128)(2,1)S(1)}, u32[]{:S(2)}, u32[]{:S(2)}) collective-permute-start(bf16[128,896]{1,0:T(8,128)(2,1)S(1)} %collective-permute-done.1.refs_2_), channel_id=1, source_target_pairs={{0,7},{1,0},{2,1},{3,2},{4,3},{5,4},{6,5},{7,6},{8,15},{9,8},{10,9... | collective-permute-start | bytes 688136 | tf_op jit(solution)/shard_map/ppermute | solution.py:303
  46.2 9.8 %collective-permute-start.11 = (bf16[128,896]{1,0:T(8,128)(2,1)S(1)}, bf16[128,896]{1,0:T(8,128)(2,1)S(1)}, u32[]{:S(2)}, u32[]{:S(2)}) collective-permute-start(bf16[128,896]{1,0:T(8,128)(2,1)S(1)} %collective-permute-done.9.refs_11_), channel_id=1, source_target_pairs={{0,7},{1,0},{2,1},{3,2},{4,3},{5,4},{6,5},{7,6},{8,15},{9,8},{10,9... | collective-permute-start | bytes 688136 | tf_op jit(solution)/shard_map/ppermute | solution.py:303
  49.4 9.8 %collective-permute-start.4 = (bf16[128,896]{1,0:T(8,128)(2,1)S(1)}, bf16[128,896]{1,0:T(8,128)(2,1)S(1)}, u32[]{:S(2)}, u32[]{:S(2)}) collective-permute-start(bf16[128,896]{1,0:T(8,128)(2,1)S(1)} %collective-permute-done.2.refs_3_), channel_id=1, source_target_pairs={{0,1},{1,2},{2,3},{3,4},{4,5},{5,6},{6,7},{7,0},{8,9},{9,10},{10,1... | collective-permute-start | bytes 688136 | tf_op jit(solution)/shard_map/ppermute | solution.py:303
  52.7 10.2 %collective-permute-start.12 = (bf16[128,896]{1,0:T(8,128)(2,1)S(1)}, bf16[128,896]{1,0:T(8,128)(2,1)S(1)}, u32[]{:S(2)}, u32[]{:S(2)}) collective-permute-start(bf16[128,896]{1,0:T(8,128)(2,1)S(1)} %collective-permute-done.10.refs_12_), channel_id=1, source_target_pairs={{0,1},{1,2},{2,3},{3,4},{4,5},{5,6},{6,7},{7,0},{8,9},{9,10},{10,1... | collective-permute-start | bytes 688136 | tf_op jit(solution)/shard_map/ppermute | solution.py:303
  52.7 10.1 %collective-permute-start.5 = (bf16[128,896]{1,0:T(8,128)(2,1)S(1)}, bf16[128,896]{1,0:T(8,128)(2,1)S(1)}, u32[]{:S(2)}, u32[]{:S(2)}) collective-permute-start(bf16[128,896]{1,0:T(8,128)(2,1)S(1)} %collective-permute-done.3.refs_4_), channel_id=1, source_target_pairs={{0,7},{1,0},{2,1},{3,2},{4,3},{5,4},{6,5},{7,6},{8,15},{9,8},{10,9... | collective-permute-start | bytes 688136 | tf_op jit(solution)/shard_map/ppermute | solution.py:303
  56.0 8.7 %collective-permute-start.13 = (bf16[128,896]{1,0:T(8,128)(2,1)S(1)}, bf16[128,896]{1,0:T(8,128)(2,1)S(1)}, u32[]{:S(2)}, u32[]{:S(2)}) collective-permute-start(bf16[128,896]{1,0:T(8,128)(2,1)S(1)} %collective-permute-done.11.refs_13_), channel_id=1, source_target_pairs={{0,7},{1,0},{2,1},{3,2},{4,3},{5,4},{6,5},{7,6},{8,15},{9,8},{10,9... | collective-permute-start | bytes 688136 | tf_op jit(solution)/shard_map/ppermute | solution.py:303
  59.2 7.9 %collective-permute-start.6 = (bf16[128,896]{1,0:T(8,128)(2,1)S(1)}, bf16[128,896]{1,0:T(8,128)(2,1)}, u32[]{:S(2)}, u32[]{:S(2)}) collective-permute-start(bf16[128,896]{1,0:T(8,128)(2,1)S(1)} %collective-permute-done.4.refs_5_), channel_id=1, source_target_pairs={{0,1},{1,2},{2,3},{3,4},{4,5},{5,6},{6,7},{7,0},{8,9},{9,10},{10,1... | collective-permute-start | bytes 688136 | tf_op jit(solution)/shard_map/ppermute | solution.py:303
  91.7 8.0 %collective-permute-start.14 = (bf16[128,896]{1,0:T(8,128)(2,1)}, bf16[128,896]{1,0:T(8,128)(2,1)S(1)}, u32[]{:S(2)}, u32[]{:S(2)}) collective-permute-start(bf16[128,896]{1,0:T(8,128)(2,1)} %get-tuple-element.27), channel_id=1, source_target_pairs={{0,1},{1,2},{2,3},{3,4},{4,5},{5,6},{6,7},{7,0},{8,9},{9,10},{10,1... | collective-permute-start | bytes 688136 | tf_op jit(solution)/shard_map/ppermute | solution.py:303
  93.7 9.7 %collective-permute-start.18 = (bf16[128,896]{1,0:T(8,128)(2,1)}, bf16[128,896]{1,0:T(8,128)(2,1)S(1)}, u32[]{:S(2)}, u32[]{:S(2)}) collective-permute-start(bf16[128,896]{1,0:T(8,128)(2,1)} %get-tuple-element.31), channel_id=1, source_target_pairs={{0,7},{1,0},{2,1},{3,2},{4,3},{5,4},{6,5},{7,6},{8,15},{9,8},{10,9... | collective-permute-start | bytes 688136 | tf_op jit(solution)/shard_map/ppermute | solution.py:303
  93.8 12.7 %collective-permute-start.21 = (bf16[128,896]{1,0:T(8,128)(2,1)}, bf16[128,896]{1,0:T(8,128)(2,1)S(1)}, u32[]{:S(2)}, u32[]{:S(2)}) collective-permute-start(bf16[128,896]{1,0:T(8,128)(2,1)} %get-tuple-element.35), channel_id=1, source_target_pairs={{0,7},{1,0},{2,1},{3,2},{4,3},{5,4},{6,5},{7,6},{8,15},{9,8},{10,9... | collective-permute-start | bytes 688136 | tf_op jit(solution)/shard_map/ppermute | solution.py:303
  97.8 13.0 %collective-permute-start.25 = (bf16[128,896]{1,0:T(8,128)(2,1)}, bf16[128,896]{1,0:T(8,128)(2,1)S(1)}, u32[]{:S(2)}, u32[]{:S(2)}) collective-permute-start(bf16[128,896]{1,0:T(8,128)(2,1)} %get-tuple-element.39), channel_id=1, source_target_pairs={{0,1},{1,2},{2,3},{3,4},{4,5},{5,6},{6,7},{7,0},{8,9},{9,10},{10,1... | collective-permute-start | bytes 688136 | tf_op jit(solution)/shard_map/ppermute | solution.py:303
  100.7 11.3 %collective-permute-start.15 = (bf16[128,896]{1,0:T(8,128)(2,1)S(1)}, bf16[128,896]{1,0:T(8,128)(2,1)S(1)}, u32[]{:S(2)}, u32[]{:S(2)}) collective-permute-start(bf16[128,896]{1,0:T(8,128)(2,1)S(1)} %add_convert_fusion.9), channel_id=1, source_target_pairs={{0,1},{1,2},{2,3},{3,4},{4,5},{5,6},{6,7},{7,0},{8,9},{9,10},{10,1... | collective-permute-start | bytes 688136 | tf_op jit(solution)/shard_map/ppermute | solution.py:303
  104.4 9.9 %collective-permute-start.19 = (bf16[128,896]{1,0:T(8,128)(2,1)S(1)}, bf16[128,896]{1,0:T(8,128)(2,1)S(1)}, u32[]{:S(2)}, u32[]{:S(2)}) collective-permute-start(bf16[128,896]{1,0:T(8,128)(2,1)S(1)} %add_convert_fusion.6), channel_id=1, source_target_pairs={{0,7},{1,0},{2,1},{3,2},{4,3},{5,4},{6,5},{7,6},{8,15},{9,8},{10,9... | collective-permute-start | bytes 688136 | tf_op jit(solution)/shard_map/ppermute | solution.py:303
  107.6 9.4 %collective-permute-start.22 = (bf16[128,896]{1,0:T(8,128)(2,1)S(1)}, bf16[128,896]{1,0:T(8,128)(2,1)S(1)}, u32[]{:S(2)}, u32[]{:S(2)}) collective-permute-start(bf16[128,896]{1,0:T(8,128)(2,1)S(1)} %add_convert_fusion.4), channel_id=1, source_target_pairs={{0,7},{1,0},{2,1},{3,2},{4,3},{5,4},{6,5},{7,6},{8,15},{9,8},{10,9... | collective-permute-start | bytes 688136 | tf_op jit(solution)/shard_map/ppermute | solution.py:303
  111.9 8.6 %collective-permute-start.26 = (bf16[128,896]{1,0:T(8,128)(2,1)S(1)}, bf16[128,896]{1,0:T(8,128)(2,1)S(1)}, u32[]{:S(2)}, u32[]{:S(2)}) collective-permute-start(bf16[128,896]{1,0:T(8,128)(2,1)S(1)} %add_convert_fusion.1), channel_id=1, source_target_pairs={{0,1},{1,2},{2,3},{3,4},{4,5},{5,6},{6,7},{7,0},{8,9},{9,10},{10,1... | collective-permute-start | bytes 688136 | tf_op jit(solution)/shard_map/ppermute | solution.py:303
  112.0 12.4 %collective-permute-start.16 = (bf16[128,896]{1,0:T(8,128)(2,1)S(1)}, bf16[128,896]{1,0:T(8,128)(2,1)S(1)}, u32[]{:S(2)}, u32[]{:S(2)}) collective-permute-start(bf16[128,896]{1,0:T(8,128)(2,1)S(1)} %add_convert_fusion.8), channel_id=1, source_target_pairs={{0,1},{1,2},{2,3},{3,4},{4,5},{5,6},{6,7},{7,0},{8,9},{9,10},{10,1... | collective-permute-start | bytes 688136 | tf_op jit(solution)/shard_map/ppermute | solution.py:303
  114.4 13.8 %collective-permute-start.20 = (bf16[128,896]{1,0:T(8,128)(2,1)S(1)}, bf16[128,896]{1,0:T(8,128)(2,1)S(1)}, u32[]{:S(2)}, u32[]{:S(2)}) collective-permute-start(bf16[128,896]{1,0:T(8,128)(2,1)S(1)} %add_convert_fusion.5), channel_id=1, source_target_pairs={{0,7},{1,0},{2,1},{3,2},{4,3},{5,4},{6,5},{7,6},{8,15},{9,8},{10,9... | collective-permute-start | bytes 688136 | tf_op jit(solution)/shard_map/ppermute | solution.py:303
  117.0 9.3 %collective-permute-start.23 = (bf16[128,896]{1,0:T(8,128)(2,1)S(1)}, bf16[128,896]{1,0:T(8,128)(2,1)S(1)}, u32[]{:S(2)}, u32[]{:S(2)}) collective-permute-start(bf16[128,896]{1,0:T(8,128)(2,1)S(1)} %add_convert_fusion.3), channel_id=1, source_target_pairs={{0,7},{1,0},{2,1},{3,2},{4,3},{5,4},{6,5},{7,6},{8,15},{9,8},{10,9... | collective-permute-start | bytes 688136 | tf_op jit(solution)/shard_map/ppermute | solution.py:303
  120.5 9.5 %collective-permute-start.27 = (bf16[128,896]{1,0:T(8,128)(2,1)S(1)}, bf16[128,896]{1,0:T(8,128)(2,1)S(1)}, u32[]{:S(2)}, u32[]{:S(2)}) collective-permute-start(bf16[128,896]{1,0:T(8,128)(2,1)S(1)} %add_convert_fusion), channel_id=1, source_target_pairs={{0,1},{1,2},{2,3},{3,4},{4,5},{5,6},{6,7},{7,0},{8,9},{9,10},{10,1... | collective-permute-start | bytes 688136 | tf_op jit(solution)/shard_map/ppermute | solution.py:303
  124.5 8.0 %collective-permute-start.17 = (bf16[128,896]{1,0:T(8,128)(2,1)S(1)}, bf16[128,896]{1,0:T(8,128)(2,1)S(1)}, u32[]{:S(2)}, u32[]{:S(2)}) collective-permute-start(bf16[128,896]{1,0:T(8,128)(2,1)S(1)} %add_convert_fusion.7), channel_id=1, source_target_pairs={{0,1},{1,2},{2,3},{3,4},{4,5},{5,6},{6,7},{7,0},{8,9},{9,10},{10,1... | collective-permute-start | bytes 688136 | tf_op jit(solution)/shard_map/ppermute | solution.py:303
  126.3 7.6 %collective-permute-start.24 = (bf16[128,896]{1,0:T(8,128)(2,1)S(1)}, bf16[128,896]{1,0:T(8,128)(2,1)S(1)}, u32[]{:S(2)}, u32[]{:S(2)}) collective-permute-start(bf16[128,896]{1,0:T(8,128)(2,1)S(1)} %add_convert_fusion.2), channel_id=1, source_target_pairs={{0,7},{1,0},{2,1},{3,2},{4,3},{5,4},{6,5},{7,6},{8,15},{9,8},{10,9... | collective-permute-start | bytes 688136 | tf_op jit(solution)/shard_map/ppermute | solution.py:303
  135.1 17.2 %all-to-all-start.2 = ((bf16[32,8,1024]{2,1,0:T(8,128)(2,1)}), bf16[32,8,1024]{2,1,0:T(8,128)(2,1)S(1)}, u32[]{:S(2)}, u32[]{:S(2)}) async-start(bf16[32,8,1024]{2,1,0:T(8,128)(2,1)} %bitcast.13), calls=%async_computation.2 | async-start | bytes 1048576 | tf_op jit(solution)/shard_map/all_to_all | solution.py:332
  (27 other events, 665.2 us)
where the time goes:
time: 184 us
  starting transfers between devices  66.6 us (36%)
  waiting for transfers between devices  47.9 us (26%)
  Pallas kernels  33.9 us (18%)
  blocking collectives  29.8 us (16%)
  other arithmetic  4.38 us (2%)
    ppermute x28, starting transfers between devices, hop(): return lax.ppermute(x, 'etp', [(i, (i + by) % N_Z) for i in range(N_Z)])  48.4 us
    ppermute x28, waiting for transfers between devices, hop(): return lax.ppermute(x, 'etp', [(i, (i + by) % N_Z) for i in range(N_Z)])  30.9 us
    all_gather x1, blocking collectives, on_device(): lax.all_gather(summed, 'etp', axis=0, tiled=False)  29.8 us
    pallas_call x1, Pallas kernels, on_device(): pl.pallas_call(functools.partial(expert_kernel, OFFSETS), out_shape=[shap...  19.5 us
    all_to_all x3, starting transfers between devices, exchange(): return lax.all_to_all(x, 'ep', split_axis=0, concat_axis=0, tiled=True)  18.2 us
    all_to_all x3, waiting for transfers between devices, exchange(): return lax.all_to_all(x, 'ep', split_axis=0, concat_axis=0, tiled=True)  17.1 us
    pallas_call x1, Pallas kernels, on_device(): pl.pallas_call(down_kernel, out_shape=shape(UNITS, D), grid=(4,), in_spec...  5.14 us
    pallas_call x1, Pallas kernels, on_device(): pl.pallas_call(send_plane_kernel, out_shape=shape(ROWS, 2 * D), in_specs=...  4.44 us
  transfers between devices with their start and end apart: 31, of which 17 were waited for; matrix products, arithmetic and copies ran while one was open for 2% of the time, Pallas kernels for 5%

commit v1 on v0

--- a/solution.py
+++ b/solution.py
@@ -146,8 +146,8 @@
             ((down_hbm, down_w), (gate_hbm, gate_w), (up_hbm, up_w))
         )
     )
-    c_x.start()
-    c_gate.start()
+    for c in (c_x, c_gate, c_up, c_rows, c_down):
+        c.start()
     by_ring = []
     for chain in range(2):
         here = pl.ds(chain * 128, 128)
@@ -172,16 +172,13 @@
 
     c_x.wait()
     c_gate.wait()
-    c_up.start()
+    for c in by_ring:
+        c.start()
     values[0] = mm(plane[0], gate_w[...], NT)
     c_up.wait()
-    c_rows.start()
-    c_down.start()
     values[1] = mm(plane[0], up_w[...], NT)
     c_rows.wait()
     c_down.wait()
-    for c in by_ring:
-        c.start()
     values[2] = mm(plane[1], down_w[...], NT)
     ahead(values[0], values[1], values[2], ROWS)
     for c in by_ring:

time: 184 us -> 182 us (0.989)
  Pallas kernels: 33.9 us -> 31.3 us
    pallas_call x1, Pallas kernels: 19.5 us -> 16.8 us  [on_device(): pl.pallas_call(functools.partial(expert_kernel, OFFSETS), out_shape=[shap...]
where the time goes in v1:
time: 182 us; the launch traced here: 181 us
  starting transfers between devices  66.6 us (37%)
  waiting for transfers between devices  47.9 us (26%)
  Pallas kernels  31.3 us (17%)
  blocking collectives  29.8 us (16%)
  other arithmetic  4.38 us (2%)
    ppermute x28, starting transfers between devices, hop(): return lax.ppermute(x, 'etp', [(i, (i + by) % N_Z) for i in range(N_Z)])  48.4 us
    ppermute x28, waiting for transfers between devices, hop(): return lax.ppermute(x, 'etp', [(i, (i + by) % N_Z) for i in range(N_Z)])  30.9 us
    all_gather x1, blocking collectives, on_device(): lax.all_gather(summed, 'etp', axis=0, tiled=False)  29.8 us
    all_to_all x3, starting transfers between devices, exchange(): return lax.all_to_all(x, 'ep', split_axis=0, concat_axis=0, tiled=True)  18.2 us
    all_to_all x3, waiting for transfers between devices, exchange(): return lax.all_to_all(x, 'ep', split_axis=0, concat_axis=0, tiled=True)  17 us
    pallas_call x1, Pallas kernels, on_device(): pl.pallas_call(functools.partial(expert_kernel, OFFSETS), out_shape=[shap...  16.8 us
    pallas_call x1, Pallas kernels, on_device(): pl.pallas_call(down_kernel, out_shape=shape(UNITS, D), grid=(4,), in_spec...  5.15 us
    pallas_call x1, Pallas kernels, on_device(): pl.pallas_call(send_plane_kernel, out_shape=shape(ROWS, 2 * D), in_specs=...  4.44 us
  transfers between devices with their start and end apart: 31, of which 17 were waited for; matrix products, arithmetic and copies ran while one was open for 2% of the time, Pallas kernels for 5%

profile of v1, /device:TPU:32, one launch (start us, length us, event | category | flops | bytes accessed | tf_op | source)
XLA Modules:
  0.0 181.2 jit_solution(17270966959666855136)
XLA Ops:
  0.6 2.1 %send_ring.1 = bf16[256,896]{1,0:T(8,128)(2,1)} custom-call(s32[1]{0:T(128)} %bitcast.2.z_ref, s32[2,128]{1,0:T(2,128)} %bitcast.24, bf16[2,128]{1,0:T(2,128)(2,1)} %bitcast.27, bf16[128,3584]{1,0:T(8,128)(2,1)} %tok_hbm.3, bf16[128,3584]{1,0:T(8,128)(2,1)} %grad_hbm.3), custom_call_target="tpu_custom_call" | custom-call | tf_op jit(solution)/shard_map/send_ring/pallas_call | solution.py:348
  2.7 7.3 %all-to-all-start = ((bf16[32,8,896]{2,1,0:T(8,128)(2,1)}), bf16[32,8,896]{2,1,0:T(8,128)(2,1)S(1)}, u32[]{:S(2)}, u32[]{:S(2)}) async-start(bf16[32,8,896]{2,1,0:T(8,128)(2,1)} %bitcast.35), calls=%async_computation | async-start | bytes 917504 | tf_op jit(solution)/shard_map/all_to_all | solution.py:329
  10.0 4.4 %send_plane.1 = bf16[256,7168]{1,0:T(8,128)(2,1)} custom-call(s32[2,128]{1,0:T(2,128)} %bitcast.25, bf16[2,128]{1,0:T(2,128)(2,1)} %bitcast.28, bf16[128,3584]{1,0:T(8,128)(2,1)} %tok_hbm.3, bf16[128,3584]{1,0:T(8,128)(2,1)} %grad_hbm.3), custom_call_target="tpu_custom_call" | custom-call | tf_op jit(solution)/shard_map/send_plane/pallas_call | solution.py:358
  14.5 6.1 %all-to-all-done = bf16[32,8,896]{2,1,0:T(8,128)(2,1)S(1)} async-done(((bf16[32,8,896]{2,1,0:T(8,128)(2,1)}), bf16[32,8,896]{2,1,0:T(8,128)(2,1)S(1)}, u32[]{:S(2)}, u32[]{:S(2)}) %all-to-all-start) | async-done | bytes 458784 | tf_op jit(solution)/shard_map/all_to_all | solution.py:329
  20.6 4.8 %all-to-all-start.1 = ((bf16[32,8,7168]{2,1,0:T(8,128)(2,1)}), bf16[32,8,7168]{2,1,0:T(8,128)(2,1)}, u32[]{:S(2)}, u32[]{:S(2)}) async-start(bf16[32,8,7168]{2,1,0:T(8,128)(2,1)} %bitcast.30), calls=%async_computation.1 | async-start | bytes 7340032 | tf_op jit(solution)/shard_map/all_to_all | solution.py:329
  27.6 1.9 %collective-permute-start.8 = (bf16[128,896]{1,0:T(8,128)(2,1)S(1)}, bf16[128,896]{1,0:T(8,128)(2,1)S(1)}, u32[]{:S(2)}, u32[]{:S(2)}) collective-permute-start(bf16[128,896]{1,0:T(8,128)(2,1)S(1)} %get-tuple-element.49.refs_8_), channel_id=1, source_target_pairs={{0,1},{1,2},{2,3},{3,4},{4,5},{5,6},{6,7},{7,0},{8,9},{9,10},{10,1... | collective-permute-start | bytes 688136 | tf_op jit(solution)/shard_map/ppermute | solution.py:300
  29.5 2.0 %collective-permute-start.1 = (bf16[128,896]{1,0:T(8,128)(2,1)S(1)}, bf16[128,896]{1,0:T(8,128)(2,1)S(1)}, u32[]{:S(2)}, u32[]{:S(2)}) collective-permute-start(bf16[128,896]{1,0:T(8,128)(2,1)S(1)} %get-tuple-element.50.refs_0_), channel_id=1, source_target_pairs={{0,7},{1,0},{2,1},{3,2},{4,3},{5,4},{6,5},{7,6},{8,15},{9,8},{10,9... | collective-permute-start | bytes 688136 | tf_op jit(solution)/shard_map/ppermute | solution.py:300
  31.5 2.5 %collective-permute-done.7.refs_9_ = bf16[128,896]{1,0:T(8,128)(2,1)S(1)} collective-permute-done((bf16[128,896]{1,0:T(8,128)(2,1)S(1)}, bf16[128,896]{1,0:T(8,128)(2,1)S(1)}, u32[]{:S(2)}, u32[]{:S(2)}) %collective-permute-start.7) | collective-permute-done | bytes 229408 | tf_op jit(solution)/shard_map/ppermute | solution.py:300
  34.0 3.4 %collective-permute-start.9 = (bf16[128,896]{1,0:T(8,128)(2,1)S(1)}, bf16[128,896]{1,0:T(8,128)(2,1)S(1)}, u32[]{:S(2)}, u32[]{:S(2)}) collective-permute-start(bf16[128,896]{1,0:T(8,128)(2,1)S(1)} %collective-permute-done.7.refs_9_), channel_id=1, source_target_pairs={{0,7},{1,0},{2,1},{3,2},{4,3},{5,4},{6,5},{7,6},{8,15},{9,8},{10,9... | collective-permute-start | bytes 688136 | tf_op jit(solution)/shard_map/ppermute | solution.py:300
  37.9 4.9 %collective-permute-done.8.refs_10_ = bf16[128,896]{1,0:T(8,128)(2,1)S(1)} collective-permute-done((bf16[128,896]{1,0:T(8,128)(2,1)S(1)}, bf16[128,896]{1,0:T(8,128)(2,1)S(1)}, u32[]{:S(2)}, u32[]{:S(2)}) %collective-permute-start.8) | collective-permute-done | bytes 229408 | tf_op jit(solution)/shard_map/ppermute | solution.py:300
  42.8 3.4 %collective-permute-start.3 = (bf16[128,896]{1,0:T(8,128)(2,1)S(1)}, bf16[128,896]{1,0:T(8,128)(2,1)S(1)}, u32[]{:S(2)}, u32[]{:S(2)}) collective-permute-start(bf16[128,896]{1,0:T(8,128)(2,1)S(1)} %collective-permute-done.1.refs_2_), channel_id=1, source_target_pairs={{0,7},{1,0},{2,1},{3,2},{4,3},{5,4},{6,5},{7,6},{8,15},{9,8},{10,9... | collective-permute-start | bytes 688136 | tf_op jit(solution)/shard_map/ppermute | solution.py:300
  46.2 3.1 %collective-permute-start.11 = (bf16[128,896]{1,0:T(8,128)(2,1)S(1)}, bf16[128,896]{1,0:T(8,128)(2,1)S(1)}, u32[]{:S(2)}, u32[]{:S(2)}) collective-permute-start(bf16[128,896]{1,0:T(8,128)(2,1)S(1)} %collective-permute-done.9.refs_11_), channel_id=1, source_target_pairs={{0,7},{1,0},{2,1},{3,2},{4,3},{5,4},{6,5},{7,6},{8,15},{9,8},{10,9... | collective-permute-start | bytes 688136 | tf_op jit(solution)/shard_map/ppermute | solution.py:300
  49.4 3.3 %collective-permute-done.10.refs_12_ = bf16[128,896]{1,0:T(8,128)(2,1)S(1)} collective-permute-done((bf16[128,896]{1,0:T(8,128)(2,1)S(1)}, bf16[128,896]{1,0:T(8,128)(2,1)S(1)}, u32[]{:S(2)}, u32[]{:S(2)}) %collective-permute-start.10) | collective-permute-done | bytes 229408 | tf_op jit(solution)/shard_map/ppermute | solution.py:300
  52.7 3.4 %collective-permute-start.5 = (bf16[128,896]{1,0:T(8,128)(2,1)S(1)}, bf16[128,896]{1,0:T(8,128)(2,1)S(1)}, u32[]{:S(2)}, u32[]{:S(2)}) collective-permute-start(bf16[128,896]{1,0:T(8,128)(2,1)S(1)} %collective-permute-done.3.refs_4_), channel_id=1, source_target_pairs={{0,7},{1,0},{2,1},{3,2},{4,3},{5,4},{6,5},{7,6},{8,15},{9,8},{10,9... | collective-permute-start | bytes 688136 | tf_op jit(solution)/shard_map/ppermute | solution.py:300
  56.0 3.1 %collective-permute-start.13 = (bf16[128,896]{1,0:T(8,128)(2,1)S(1)}, bf16[128,896]{1,0:T(8,128)(2,1)S(1)}, u32[]{:S(2)}, u32[]{:S(2)}) collective-permute-start(bf16[128,896]{1,0:T(8,128)(2,1)S(1)} %collective-permute-done.11.refs_13_), channel_id=1, source_target_pairs={{0,7},{1,0},{2,1},{3,2},{4,3},{5,4},{6,5},{7,6},{8,15},{9,8},{10,9... | collective-permute-start | bytes 688136 | tf_op jit(solution)/shard_map/ppermute | solution.py:300
  59.2 3.6 %collective-permute-done.12.refs_14_ = bf16[128,896]{1,0:T(8,128)(2,1)S(1)} collective-permute-done((bf16[128,896]{1,0:T(8,128)(2,1)S(1)}, bf16[128,896]{1,0:T(8,128)(2,1)S(1)}, u32[]{:S(2)}, u32[]{:S(2)}) %collective-permute-start.12) | collective-permute-done | bytes 229408 | tf_op jit(solution)/shard_map/ppermute | solution.py:300
  64.7 2.4 %collective-permute-done.6.refs_7_ = bf16[128,896]{1,0:T(8,128)(2,1)} collective-permute-done((bf16[128,896]{1,0:T(8,128)(2,1)S(1)}, bf16[128,896]{1,0:T(8,128)(2,1)}, u32[]{:S(2)}, u32[]{:S(2)}) %collective-permute-start.6) | collective-permute-done | bytes 229408 | tf_op jit(solution)/shard_map/ppermute | solution.py:300
  67.1 5.0 %all-to-all-done.1 = bf16[32,8,7168]{2,1,0:T(8,128)(2,1)} async-done(((bf16[32,8,7168]{2,1,0:T(8,128)(2,1)}), bf16[32,8,7168]{2,1,0:T(8,128)(2,1)}, u32[]{:S(2)}, u32[]{:S(2)}) %all-to-all-start.1) | async-done | bytes 3670048 | tf_op jit(solution)/shard_map/all_to_all | solution.py:329
  72.2 16.8 %expert.1 = (bf16[128,896]{1,0:T(8,128)(2,1)}, bf16[128,896]{1,0:T(8,128)(2,1)}, bf16[128,896]{1,0:T(8,128)(2,1)}, bf16[128,896]{1,0:T(8,128)(2,1)}, bf16[128,89...) custom-call(s32[1]{0:T(128)} %bitcast.2.z_ref, ...), custom_call_target="tpu_custom_call" | custom-call | tf_op jit(solution)/shard_map/expert/pallas_call | solution.py:372
  89.1 2.0 %collective-permute-start.14 = (bf16[128,896]{1,0:T(8,128)(2,1)}, bf16[128,896]{1,0:T(8,128)(2,1)S(1)}, u32[]{:S(2)}, u32[]{:S(2)}) collective-permute-start(bf16[128,896]{1,0:T(8,128)(2,1)} %get-tuple-element.27), channel_id=1, source_target_pairs={{0,1},{1,2},{2,3},{3,4},{4,5},{5,6},{6,7},{7,0},{8,9},{9,10},{10,1... | collective-permute-start | bytes 688136 | tf_op jit(solution)/shard_map/ppermute | solution.py:300
  91.2 4.0 %collective-permute-start.21 = (bf16[128,896]{1,0:T(8,128)(2,1)}, bf16[128,896]{1,0:T(8,128)(2,1)S(1)}, u32[]{:S(2)}, u32[]{:S(2)}) collective-permute-start(bf16[128,896]{1,0:T(8,128)(2,1)} %get-tuple-element.35), channel_id=1, source_target_pairs={{0,7},{1,0},{2,1},{3,2},{4,3},{5,4},{6,5},{7,6},{8,15},{9,8},{10,9... | collective-permute-start | bytes 688136 | tf_op jit(solution)/shard_map/ppermute | solution.py:300
  98.0 2.7 %collective-permute-start.15 = (bf16[128,896]{1,0:T(8,128)(2,1)S(1)}, bf16[128,896]{1,0:T(8,128)(2,1)S(1)}, u32[]{:S(2)}, u32[]{:S(2)}) collective-permute-start(bf16[128,896]{1,0:T(8,128)(2,1)S(1)} %add_convert_fusion.9), channel_id=1, source_target_pairs={{0,1},{1,2},{2,3},{3,4},{4,5},{5,6},{6,7},{7,0},{8,9},{9,10},{10,1... | collective-permute-start | bytes 688136 | tf_op jit(solution)/shard_map/ppermute | solution.py:300
  101.8 2.1 %collective-permute-start.19 = (bf16[128,896]{1,0:T(8,128)(2,1)S(1)}, bf16[128,896]{1,0:T(8,128)(2,1)S(1)}, u32[]{:S(2)}, u32[]{:S(2)}) collective-permute-start(bf16[128,896]{1,0:T(8,128)(2,1)S(1)} %add_convert_fusion.6), channel_id=1, source_target_pairs={{0,7},{1,0},{2,1},{3,2},{4,3},{5,4},{6,5},{7,6},{8,15},{9,8},{10,9... | collective-permute-start | bytes 688136 | tf_op jit(solution)/shard_map/ppermute | solution.py:300
  104.9 3.3 %collective-permute-start.22 = (bf16[128,896]{1,0:T(8,128)(2,1)S(1)}, bf16[128,896]{1,0:T(8,128)(2,1)S(1)}, u32[]{:S(2)}, u32[]{:S(2)}) collective-permute-start(bf16[128,896]{1,0:T(8,128)(2,1)S(1)} %add_convert_fusion.4), channel_id=1, source_target_pairs={{0,7},{1,0},{2,1},{3,2},{4,3},{5,4},{6,5},{7,6},{8,15},{9,8},{10,9... | collective-permute-start | bytes 688136 | tf_op jit(solution)/shard_map/ppermute | solution.py:300
  109.4 2.3 %collective-permute-start.16 = (bf16[128,896]{1,0:T(8,128)(2,1)S(1)}, bf16[128,896]{1,0:T(8,128)(2,1)S(1)}, u32[]{:S(2)}, u32[]{:S(2)}) collective-permute-start(bf16[128,896]{1,0:T(8,128)(2,1)S(1)} %add_convert_fusion.8), channel_id=1, source_target_pairs={{0,1},{1,2},{2,3},{3,4},{4,5},{5,6},{6,7},{7,0},{8,9},{9,10},{10,1... | collective-permute-start | bytes 688136 | tf_op jit(solution)/shard_map/ppermute | solution.py:300
  114.3 3.5 %collective-permute-start.23 = (bf16[128,896]{1,0:T(8,128)(2,1)S(1)}, bf16[128,896]{1,0:T(8,128)(2,1)S(1)}, u32[]{:S(2)}, u32[]{:S(2)}) collective-permute-start(bf16[128,896]{1,0:T(8,128)(2,1)S(1)} %add_convert_fusion.3), channel_id=1, source_target_pairs={{0,7},{1,0},{2,1},{3,2},{4,3},{5,4},{6,5},{7,6},{8,15},{9,8},{10,9... | collective-permute-start | bytes 688136 | tf_op jit(solution)/shard_map/ppermute | solution.py:300
  119.2 2.7 %collective-permute-done.16 = bf16[128,896]{1,0:T(8,128)(2,1)S(1)} collective-permute-done((bf16[128,896]{1,0:T(8,128)(2,1)S(1)}, bf16[128,896]{1,0:T(8,128)(2,1)S(1)}, u32[]{:S(2)}, u32[]{:S(2)}) %collective-permute-start.16) | collective-permute-done | bytes 229408 | tf_op jit(solution)/shard_map/ppermute | solution.py:300
  127.4 2.5 %collective-permute-done.17.refs_1_ = bf16[128,896]{1,0:T(8,128)(2,1)S(1)} collective-permute-done((bf16[128,896]{1,0:T(8,128)(2,1)S(1)}, bf16[128,896]{1,0:T(8,128)(2,1)S(1)}, u32[]{:S(2)}, u32[]{:S(2)}) %collective-permute-start.17) | collective-permute-done | bytes 229408 | tf_op jit(solution)/shard_map/ppermute | solution.py:300
  132.4 6.0 %all-to-all-start.2 = ((bf16[32,8,1024]{2,1,0:T(8,128)(2,1)}), bf16[32,8,1024]{2,1,0:T(8,128)(2,1)S(1)}, u32[]{:S(2)}, u32[]{:S(2)}) async-start(bf16[32,8,1024]{2,1,0:T(8,128)(2,1)} %bitcast.13), calls=%async_computation.2 | async-start | bytes 1048576 | tf_op jit(solution)/shard_map/all_to_all | solution.py:329
  138.5 5.1 %down_grad.1 = bf16[400,3584]{1,0:T(8,128)(2,1)} custom-call(bf16[512,400]{1,0:T(8,128)(2,1)S(1)} %copy-done.1, bf16[256,3584]{1,0:T(8,128)(2,1)S(1)} %copy-done, bf16[256,7168]{1,0:T(8,128)(2,1)} %bitcast.7.refs_16_.rows1), custom_call_target="tpu_custom_call" | custom-call | tf_op jit(solution)/shard_map/down_grad/pallas_call | solution.py:412
  143.7 6.0 %all-to-all-done.2 = bf16[32,8,1024]{2,1,0:T(8,128)(2,1)S(1)} async-done(((bf16[32,8,1024]{2,1,0:T(8,128)(2,1)}), bf16[32,8,1024]{2,1,0:T(8,128)(2,1)S(1)}, u32[]{:S(2)}, u32[]{:S(2)}) %all-to-all-start.2) | async-done | bytes 524320 | tf_op jit(solution)/shard_map/all_to_all | solution.py:329
  150.3 29.8 %all-gather = bf16[3712,128]{1,0:T(8,128)(2,1)S(1)} all-gather(bf16[464,128]{1,0:T(8,128)(2,1)S(1)} %token_sum.1), channel_id=2, replica_groups=mesh['ep'=32,'etp'=8] {'etp'}, dimensions={0}, use_global_device_ids=true | all-gather | bytes 1069056 | tf_op jit(solution)/shard_map/all_gather | solution.py:441
  (105 shorter events, 24.6 us)
Async XLA Ops:
  2.7 17.9 %all-to-all-start = ((bf16[32,8,896]{2,1,0:T(8,128)(2,1)}), bf16[32,8,896]{2,1,0:T(8,128)(2,1)S(1)}, u32[]{:S(2)}, u32[]{:S(2)}) async-start(bf16[32,8,896]{2,1,0:T(8,128)(2,1)} %bitcast.35), calls=%async_computation | async-start | bytes 917504 | tf_op jit(solution)/shard_map/all_to_all | solution.py:329
  20.6 51.5 %all-to-all-start.1 = ((bf16[32,8,7168]{2,1,0:T(8,128)(2,1)}), bf16[32,8,7168]{2,1,0:T(8,128)(2,1)}, u32[]{:S(2)}, u32[]{:S(2)}) async-start(bf16[32,8,7168]{2,1,0:T(8,128)(2,1)} %bitcast.30), calls=%async_computation.1 | async-start | bytes 7340032 | tf_op jit(solution)/shard_map/all_to_all | solution.py:329
  25.5 46.6 %copy-start.7 = (bf16[128,896]{1,0:T(8,128)(2,1)}, bf16[128,896]{1,0:T(8,128)(2,1)S(1)}, u32[]{:S(2)}) copy-start(bf16[128,896]{1,0:T(8,128)(2,1)S(1)} %get-tuple-element.49.refs_8_) | copy-start | bytes 688132
  25.5 8.6 %collective-permute-start.7 = (bf16[128,896]{1,0:T(8,128)(2,1)S(1)}, bf16[128,896]{1,0:T(8,128)(2,1)S(1)}, u32[]{:S(2)}, u32[]{:S(2)}) collective-permute-start(bf16[128,896]{1,0:T(8,128)(2,1)S(1)} %get-tuple-element.49.refs_8_), channel_id=1, source_target_pairs={{0,7},{1,0},{2,1},{3,2},{4,3},{5,4},{6,5},{7,6},{8,15},{9,8},{10,9... | collective-permute-start | bytes 688136 | tf_op jit(solution)/shard_map/ppermute | solution.py:300
  25.7 12.2 %collective-permute-start = (bf16[128,896]{1,0:T(8,128)(2,1)S(1)}, bf16[128,896]{1,0:T(8,128)(2,1)S(1)}, u32[]{:S(2)}, u32[]{:S(2)}) collective-permute-start(bf16[128,896]{1,0:T(8,128)(2,1)S(1)} %get-tuple-element.50.refs_0_), channel_id=1, source_target_pairs={{0,1},{1,2},{2,3},{3,4},{4,5},{5,6},{6,7},{7,0},{8,9},{9,10},{10,1... | collective-permute-start | bytes 688136 | tf_op jit(solution)/shard_map/ppermute | solution.py:300
  27.6 15.2 %collective-permute-start.8 = (bf16[128,896]{1,0:T(8,128)(2,1)S(1)}, bf16[128,896]{1,0:T(8,128)(2,1)S(1)}, u32[]{:S(2)}, u32[]{:S(2)}) collective-permute-start(bf16[128,896]{1,0:T(8,128)(2,1)S(1)} %get-tuple-element.49.refs_8_), channel_id=1, source_target_pairs={{0,1},{1,2},{2,3},{3,4},{4,5},{5,6},{6,7},{7,0},{8,9},{9,10},{10,1... | collective-permute-start | bytes 688136 | tf_op jit(solution)/shard_map/ppermute | solution.py:300
  29.5 13.3 %collective-permute-start.1 = (bf16[128,896]{1,0:T(8,128)(2,1)S(1)}, bf16[128,896]{1,0:T(8,128)(2,1)S(1)}, u32[]{:S(2)}, u32[]{:S(2)}) collective-permute-start(bf16[128,896]{1,0:T(8,128)(2,1)S(1)} %get-tuple-element.50.refs_0_), channel_id=1, source_target_pairs={{0,7},{1,0},{2,1},{3,2},{4,3},{5,4},{6,5},{7,6},{8,15},{9,8},{10,9... | collective-permute-start | bytes 688136 | tf_op jit(solution)/shard_map/ppermute | solution.py:300
  34.0 12.2 %collective-permute-start.9 = (bf16[128,896]{1,0:T(8,128)(2,1)S(1)}, bf16[128,896]{1,0:T(8,128)(2,1)S(1)}, u32[]{:S(2)}, u32[]{:S(2)}) collective-permute-start(bf16[128,896]{1,0:T(8,128)(2,1)S(1)} %collective-permute-done.7.refs_9_), channel_id=1, source_target_pairs={{0,7},{1,0},{2,1},{3,2},{4,3},{5,4},{6,5},{7,6},{8,15},{9,8},{10,9... | collective-permute-start | bytes 688136 | tf_op jit(solution)/shard_map/ppermute | solution.py:300
  37.9 11.4 %collective-permute-start.2 = (bf16[128,896]{1,0:T(8,128)(2,1)S(1)}, bf16[128,896]{1,0:T(8,128)(2,1)S(1)}, u32[]{:S(2)}, u32[]{:S(2)}) collective-permute-start(bf16[128,896]{1,0:T(8,128)(2,1)S(1)} %collective-permute-done.refs_1_), channel_id=1, source_target_pairs={{0,1},{1,2},{2,3},{3,4},{4,5},{5,6},{6,7},{7,0},{8,9},{9,10},{10,1... | collective-permute-start | bytes 688136 | tf_op jit(solution)/shard_map/ppermute | solution.py:300
  42.8 9.8 %collective-permute-start.10 = (bf16[128,896]{1,0:T(8,128)(2,1)S(1)}, bf16[128,896]{1,0:T(8,128)(2,1)S(1)}, u32[]{:S(2)}, u32[]{:S(2)}) collective-permute-start(bf16[128,896]{1,0:T(8,128)(2,1)S(1)} %collective-permute-done.8.refs_10_), channel_id=1, source_target_pairs={{0,1},{1,2},{2,3},{3,4},{4,5},{5,6},{6,7},{7,0},{8,9},{9,10},{10,1... | collective-permute-start | bytes 688136 | tf_op jit(solution)/shard_map/ppermute | solution.py:300
  42.8 9.8 %collective-permute-start.3 = (bf16[128,896]{1,0:T(8,128)(2,1)S(1)}, bf16[128,896]{1,0:T(8,128)(2,1)S(1)}, u32[]{:S(2)}, u32[]{:S(2)}) collective-permute-start(bf16[128,896]{1,0:T(8,128)(2,1)S(1)} %collective-permute-done.1.refs_2_), channel_id=1, source_target_pairs={{0,7},{1,0},{2,1},{3,2},{4,3},{5,4},{6,5},{7,6},{8,15},{9,8},{10,9... | collective-permute-start | bytes 688136 | tf_op jit(solution)/shard_map/ppermute | solution.py:300
  46.2 9.8 %collective-permute-start.11 = (bf16[128,896]{1,0:T(8,128)(2,1)S(1)}, bf16[128,896]{1,0:T(8,128)(2,1)S(1)}, u32[]{:S(2)}, u32[]{:S(2)}) collective-permute-start(bf16[128,896]{1,0:T(8,128)(2,1)S(1)} %collective-permute-done.9.refs_11_), channel_id=1, source_target_pairs={{0,7},{1,0},{2,1},{3,2},{4,3},{5,4},{6,5},{7,6},{8,15},{9,8},{10,9... | collective-permute-start | bytes 688136 | tf_op jit(solution)/shard_map/ppermute | solution.py:300
  49.4 9.8 %collective-permute-start.4 = (bf16[128,896]{1,0:T(8,128)(2,1)S(1)}, bf16[128,896]{1,0:T(8,128)(2,1)S(1)}, u32[]{:S(2)}, u32[]{:S(2)}) collective-permute-start(bf16[128,896]{1,0:T(8,128)(2,1)S(1)} %collective-permute-done.2.refs_3_), channel_id=1, source_target_pairs={{0,1},{1,2},{2,3},{3,4},{4,5},{5,6},{6,7},{7,0},{8,9},{9,10},{10,1... | collective-permute-start | bytes 688136 | tf_op jit(solution)/shard_map/ppermute | solution.py:300
  52.7 10.2 %collective-permute-start.12 = (bf16[128,896]{1,0:T(8,128)(2,1)S(1)}, bf16[128,896]{1,0:T(8,128)(2,1)S(1)}, u32[]{:S(2)}, u32[]{:S(2)}) collective-permute-start(bf16[128,896]{1,0:T(8,128)(2,1)S(1)} %collective-permute-done.10.refs_12_), channel_id=1, source_target_pairs={{0,1},{1,2},{2,3},{3,4},{4,5},{5,6},{6,7},{7,0},{8,9},{9,10},{10,1... | collective-permute-start | bytes 688136 | tf_op jit(solution)/shard_map/ppermute | solution.py:300
  52.7 10.1 %collective-permute-start.5 = (bf16[128,896]{1,0:T(8,128)(2,1)S(1)}, bf16[128,896]{1,0:T(8,128)(2,1)S(1)}, u32[]{:S(2)}, u32[]{:S(2)}) collective-permute-start(bf16[128,896]{1,0:T(8,128)(2,1)S(1)} %collective-permute-done.3.refs_4_), channel_id=1, source_target_pairs={{0,7},{1,0},{2,1},{3,2},{4,3},{5,4},{6,5},{7,6},{8,15},{9,8},{10,9... | collective-permute-start | bytes 688136 | tf_op jit(solution)/shard_map/ppermute | solution.py:300
  56.0 8.7 %collective-permute-start.13 = (bf16[128,896]{1,0:T(8,128)(2,1)S(1)}, bf16[128,896]{1,0:T(8,128)(2,1)S(1)}, u32[]{:S(2)}, u32[]{:S(2)}) collective-permute-start(bf16[128,896]{1,0:T(8,128)(2,1)S(1)} %collective-permute-done.11.refs_13_), channel_id=1, source_target_pairs={{0,7},{1,0},{2,1},{3,2},{4,3},{5,4},{6,5},{7,6},{8,15},{9,8},{10,9... | collective-permute-start | bytes 688136 | tf_op jit(solution)/shard_map/ppermute | solution.py:300
  59.2 7.9 %collective-permute-start.6 = (bf16[128,896]{1,0:T(8,128)(2,1)S(1)}, bf16[128,896]{1,0:T(8,128)(2,1)}, u32[]{:S(2)}, u32[]{:S(2)}) collective-permute-start(bf16[128,896]{1,0:T(8,128)(2,1)S(1)} %collective-permute-done.4.refs_5_), channel_id=1, source_target_pairs={{0,1},{1,2},{2,3},{3,4},{4,5},{5,6},{6,7},{7,0},{8,9},{9,10},{10,1... | collective-permute-start | bytes 688136 | tf_op jit(solution)/shard_map/ppermute | solution.py:300
  89.1 8.0 %collective-permute-start.14 = (bf16[128,896]{1,0:T(8,128)(2,1)}, bf16[128,896]{1,0:T(8,128)(2,1)S(1)}, u32[]{:S(2)}, u32[]{:S(2)}) collective-permute-start(bf16[128,896]{1,0:T(8,128)(2,1)} %get-tuple-element.27), channel_id=1, source_target_pairs={{0,1},{1,2},{2,3},{3,4},{4,5},{5,6},{6,7},{7,0},{8,9},{9,10},{10,1... | collective-permute-start | bytes 688136 | tf_op jit(solution)/shard_map/ppermute | solution.py:300
  91.1 9.7 %collective-permute-start.18 = (bf16[128,896]{1,0:T(8,128)(2,1)}, bf16[128,896]{1,0:T(8,128)(2,1)S(1)}, u32[]{:S(2)}, u32[]{:S(2)}) collective-permute-start(bf16[128,896]{1,0:T(8,128)(2,1)} %get-tuple-element.31), channel_id=1, source_target_pairs={{0,7},{1,0},{2,1},{3,2},{4,3},{5,4},{6,5},{7,6},{8,15},{9,8},{10,9... | collective-permute-start | bytes 688136 | tf_op jit(solution)/shard_map/ppermute | solution.py:300
  91.2 12.7 %collective-permute-start.21 = (bf16[128,896]{1,0:T(8,128)(2,1)}, bf16[128,896]{1,0:T(8,128)(2,1)S(1)}, u32[]{:S(2)}, u32[]{:S(2)}) collective-permute-start(bf16[128,896]{1,0:T(8,128)(2,1)} %get-tuple-element.35), channel_id=1, source_target_pairs={{0,7},{1,0},{2,1},{3,2},{4,3},{5,4},{6,5},{7,6},{8,15},{9,8},{10,9... | collective-permute-start | bytes 688136 | tf_op jit(solution)/shard_map/ppermute | solution.py:300
  95.2 13.0 %collective-permute-start.25 = (bf16[128,896]{1,0:T(8,128)(2,1)}, bf16[128,896]{1,0:T(8,128)(2,1)S(1)}, u32[]{:S(2)}, u32[]{:S(2)}) collective-permute-start(bf16[128,896]{1,0:T(8,128)(2,1)} %get-tuple-element.39), channel_id=1, source_target_pairs={{0,1},{1,2},{2,3},{3,4},{4,5},{5,6},{6,7},{7,0},{8,9},{9,10},{10,1... | collective-permute-start | bytes 688136 | tf_op jit(solution)/shard_map/ppermute | solution.py:300
  98.0 11.3 %collective-permute-start.15 = (bf16[128,896]{1,0:T(8,128)(2,1)S(1)}, bf16[128,896]{1,0:T(8,128)(2,1)S(1)}, u32[]{:S(2)}, u32[]{:S(2)}) collective-permute-start(bf16[128,896]{1,0:T(8,128)(2,1)S(1)} %add_convert_fusion.9), channel_id=1, source_target_pairs={{0,1},{1,2},{2,3},{3,4},{4,5},{5,6},{6,7},{7,0},{8,9},{9,10},{10,1... | collective-permute-start | bytes 688136 | tf_op jit(solution)/shard_map/ppermute | solution.py:300
  101.8 9.9 %collective-permute-start.19 = (bf16[128,896]{1,0:T(8,128)(2,1)S(1)}, bf16[128,896]{1,0:T(8,128)(2,1)S(1)}, u32[]{:S(2)}, u32[]{:S(2)}) collective-permute-start(bf16[128,896]{1,0:T(8,128)(2,1)S(1)} %add_convert_fusion.6), channel_id=1, source_target_pairs={{0,7},{1,0},{2,1},{3,2},{4,3},{5,4},{6,5},{7,6},{8,15},{9,8},{10,9... | collective-permute-start | bytes 688136 | tf_op jit(solution)/shard_map/ppermute | solution.py:300
  104.9 9.4 %collective-permute-start.22 = (bf16[128,896]{1,0:T(8,128)(2,1)S(1)}, bf16[128,896]{1,0:T(8,128)(2,1)S(1)}, u32[]{:S(2)}, u32[]{:S(2)}) collective-permute-start(bf16[128,896]{1,0:T(8,128)(2,1)S(1)} %add_convert_fusion.4), channel_id=1, source_target_pairs={{0,7},{1,0},{2,1},{3,2},{4,3},{5,4},{6,5},{7,6},{8,15},{9,8},{10,9... | collective-permute-start | bytes 688136 | tf_op jit(solution)/shard_map/ppermute | solution.py:300
  109.2 8.6 %collective-permute-start.26 = (bf16[128,896]{1,0:T(8,128)(2,1)S(1)}, bf16[128,896]{1,0:T(8,128)(2,1)S(1)}, u32[]{:S(2)}, u32[]{:S(2)}) collective-permute-start(bf16[128,896]{1,0:T(8,128)(2,1)S(1)} %add_convert_fusion.1), channel_id=1, source_target_pairs={{0,1},{1,2},{2,3},{3,4},{4,5},{5,6},{6,7},{7,0},{8,9},{9,10},{10,1... | collective-permute-start | bytes 688136 | tf_op jit(solution)/shard_map/ppermute | solution.py:300
  109.4 12.4 %collective-permute-start.16 = (bf16[128,896]{1,0:T(8,128)(2,1)S(1)}, bf16[128,896]{1,0:T(8,128)(2,1)S(1)}, u32[]{:S(2)}, u32[]{:S(2)}) collective-permute-start(bf16[128,896]{1,0:T(8,128)(2,1)S(1)} %add_convert_fusion.8), channel_id=1, source_target_pairs={{0,1},{1,2},{2,3},{3,4},{4,5},{5,6},{6,7},{7,0},{8,9},{9,10},{10,1... | collective-permute-start | bytes 688136 | tf_op jit(solution)/shard_map/ppermute | solution.py:300
  111.7 13.8 %collective-permute-start.20 = (bf16[128,896]{1,0:T(8,128)(2,1)S(1)}, bf16[128,896]{1,0:T(8,128)(2,1)S(1)}, u32[]{:S(2)}, u32[]{:S(2)}) collective-permute-start(bf16[128,896]{1,0:T(8,128)(2,1)S(1)} %add_convert_fusion.5), channel_id=1, source_target_pairs={{0,7},{1,0},{2,1},{3,2},{4,3},{5,4},{6,5},{7,6},{8,15},{9,8},{10,9... | collective-permute-start | bytes 688136 | tf_op jit(solution)/shard_map/ppermute | solution.py:300
  114.3 9.3 %collective-permute-start.23 = (bf16[128,896]{1,0:T(8,128)(2,1)S(1)}, bf16[128,896]{1,0:T(8,128)(2,1)S(1)}, u32[]{:S(2)}, u32[]{:S(2)}) collective-permute-start(bf16[128,896]{1,0:T(8,128)(2,1)S(1)} %add_convert_fusion.3), channel_id=1, source_target_pairs={{0,7},{1,0},{2,1},{3,2},{4,3},{5,4},{6,5},{7,6},{8,15},{9,8},{10,9... | collective-permute-start | bytes 688136 | tf_op jit(solution)/shard_map/ppermute | solution.py:300
  117.9 9.5 %collective-permute-start.27 = (bf16[128,896]{1,0:T(8,128)(2,1)S(1)}, bf16[128,896]{1,0:T(8,128)(2,1)S(1)}, u32[]{:S(2)}, u32[]{:S(2)}) collective-permute-start(bf16[128,896]{1,0:T(8,128)(2,1)S(1)} %add_convert_fusion), channel_id=1, source_target_pairs={{0,1},{1,2},{2,3},{3,4},{4,5},{5,6},{6,7},{7,0},{8,9},{9,10},{10,1... | collective-permute-start | bytes 688136 | tf_op jit(solution)/shard_map/ppermute | solution.py:300
  121.9 8.0 %collective-permute-start.17 = (bf16[128,896]{1,0:T(8,128)(2,1)S(1)}, bf16[128,896]{1,0:T(8,128)(2,1)S(1)}, u32[]{:S(2)}, u32[]{:S(2)}) collective-permute-start(bf16[128,896]{1,0:T(8,128)(2,1)S(1)} %add_convert_fusion.7), channel_id=1, source_target_pairs={{0,1},{1,2},{2,3},{3,4},{4,5},{5,6},{6,7},{7,0},{8,9},{9,10},{10,1... | collective-permute-start | bytes 688136 | tf_op jit(solution)/shard_map/ppermute | solution.py:300
  123.7 7.6 %collective-permute-start.24 = (bf16[128,896]{1,0:T(8,128)(2,1)S(1)}, bf16[128,896]{1,0:T(8,128)(2,1)S(1)}, u32[]{:S(2)}, u32[]{:S(2)}) collective-permute-start(bf16[128,896]{1,0:T(8,128)(2,1)S(1)} %add_convert_fusion.2), channel_id=1, source_target_pairs={{0,7},{1,0},{2,1},{3,2},{4,3},{5,4},{6,5},{7,6},{8,15},{9,8},{10,9... | collective-permute-start | bytes 688136 | tf_op jit(solution)/shard_map/ppermute | solution.py:300
  132.4 17.2 %all-to-all-start.2 = ((bf16[32,8,1024]{2,1,0:T(8,128)(2,1)}), bf16[32,8,1024]{2,1,0:T(8,128)(2,1)S(1)}, u32[]{:S(2)}, u32[]{:S(2)}) async-start(bf16[32,8,1024]{2,1,0:T(8,128)(2,1)} %bitcast.13), calls=%async_computation.2 | async-start | bytes 1048576 | tf_op jit(solution)/shard_map/all_to_all | solution.py:329
  (27 other events, 665.4 us)
